TPU v7x, 256 devices: a whole 4x4x8 slice. The times are simulated.
256 devices in a mesh: lon: 32 (over x_lo, z, core), lat: 8 (over x_hi, y).
Axes of the slice: x: 4 (x_hi: 2, x_lo: 2; x = x_hi * 2 + x_lo), y: 4, z: 8, core: 2. Of those that a mesh axis runs over, the one named last changes fastest.
Arguments:
- tokens: bfloat16 [4, 48, 384, 512], P(None, 'lat', 'lon'), may hold values from -45 to 45
- gain_attn: float32 [512], replicated, may hold values from 0.1 to 1.9
- w_qkv: bfloat16 [512, 1536], replicated, may hold values from -8 to 8
- w_out: bfloat16 [512, 512], replicated, may hold values from -0.25 to 0.25
- gain_mlp: float32 [512], replicated, may hold values from 0.1 to 1.9
- w_up: bfloat16 [512, 2048], replicated, may hold values from -0.25 to 0.25
- w_down: bfloat16 [2048, 512], replicated, may hold values from -0.125 to 0.125
Outputs:
- block_out: bfloat16 [4, 48, 384, 512], P(None, 'lat', 'lon')
All inputs are finite; a program needn't handle non-finite values.
Results may differ from a plain program's by a relative error of at most 0.014.
The roundings to bfloat16 on the way count: a program that leaves them out, or rounds other values in their place, can miss the bound.
Values may be sent and summed in bfloat16 or wider, within the bound.
A program may use at most 128 MiB of HBM per device.

v0:
```python
import jax
import jax.numpy as jnp
from jax import lax
from jax.sharding import PartitionSpec as P

HEADS = 8


def shifted_2(value, axis, steps):
    count = lax.axis_size(axis)
    pairs = [(source, (source + steps) % count) for source in range(count)]
    return lax.ppermute(value, axis, pairs)


def layer_norm(values, gain_vec):
    values = values.astype(jnp.float32)
    average = jnp.mean(values, axis=-1, keepdims=True)
    centered = values - average
    spread = jnp.mean(centered * centered, axis=-1, keepdims=True)
    return centered * lax.rsqrt(spread + 1e-05) * gain_vec


def split_windows(tile_block):
    levels, lat_rows, lon_cols, features = tile_block.shape
    parted = tile_block.reshape(levels // 2, 2, lat_rows // 6, 6, lon_cols // 12, 12, features)
    parted = parted.transpose(0, 2, 4, 1, 3, 5, 6)
    return parted.reshape(-1, 144, features)


def merge_windows(parted, levels, lat_rows, lon_cols):
    features = parted.shape[-1]
    tile_block = parted.reshape(levels // 2, lat_rows // 6, lon_cols // 12, 2, 6, 12, features)
    tile_block = tile_block.transpose(0, 3, 1, 4, 2, 5, 6)
    return tile_block.reshape(levels, lat_rows, lon_cols, features)


def token_keys(key_table, lon_cols):
    levels, lat_rows = key_table.shape
    widened = jnp.broadcast_to(key_table[:, :, None, None], (levels, lat_rows, lon_cols, 1))
    return split_windows(widened)[..., 0]


def window_mask(level_table, row_table, usable, lon_cols):
    allowed = None
    for key_table in (level_table, row_table):
        window_key = token_keys(key_table, lon_cols)
        agrees = window_key[:, :, None] == window_key[:, None, :]
        allowed = agrees if allowed is None else allowed & agrees
    return allowed & (token_keys(usable, lon_cols)[:, None, :] > 0.5)


def head_attention(query_part, key_part, value_part, allowed, w_out_rows):
    head_dim = query_part.shape[-1]
    scores = jnp.einsum(
        "wqd,wkd->wqk", query_part, key_part, preferred_element_type=jnp.float32
    ) * head_dim ** (-0.5)
    scores = jnp.where(allowed, scores, -1e30)
    ceiling = jnp.max(scores, axis=-1, keepdims=True)
    raised = jnp.exp(scores - ceiling)
    weights = (raised / jnp.sum(raised, axis=-1, keepdims=True)).astype(jnp.bfloat16)
    attended = jnp.einsum(
        "wqk,wkd->wqd", weights, value_part, preferred_element_type=jnp.float32
    ).astype(jnp.bfloat16)
    return jnp.dot(attended, w_out_rows, preferred_element_type=jnp.float32)


def level_keys(levels, row_count):
    level_order = (jnp.arange(levels) + 1) % levels
    return jnp.broadcast_to(
        ((level_order + 1) // 2).astype(jnp.float32)[:, None], (levels, row_count)
    )


def body(tokens, gain_attn, w_qkv, w_out, gain_mlp, w_up, w_down):
    levels, lat_rows, lon_cols, features = tokens.shape
    head_dim = features // HEADS
    lat_index = lax.axis_index("lat")
    total_rows = lat_rows * lax.axis_size("lat")
    edge_cols = shifted_2(tokens[:, :, :6], "lon", -1)
    shifted = jnp.concatenate([tokens[:, :, 6:], edge_cols], axis=2)
    edge_rows = shifted_2(shifted[:, :3], "lat", -1)
    shifted = jnp.concatenate([shifted[:, 3:], edge_rows], axis=1)
    shifted = jnp.roll(shifted, -1, axis=0)
    global_rows = (lat_index * lat_rows + jnp.arange(lat_rows) + 3) % total_rows
    row_table = jnp.broadcast_to(
        ((global_rows + 3) // 6).astype(jnp.float32)[None, :], (levels, lat_rows)
    )
    usable = jnp.ones((levels, lat_rows), jnp.float32)
    allowed = window_mask(level_keys(levels, lat_rows), row_table, usable, lon_cols)
    normed_win = layer_norm(split_windows(shifted), gain_attn).astype(jnp.bfloat16)
    mixed_win = None
    for head in range(HEADS):
        low = head * head_dim
        query_part = jnp.dot(
            normed_win, w_qkv[:, low : low + head_dim], preferred_element_type=jnp.float32
        ).astype(jnp.bfloat16)
        key_part = jnp.dot(
            normed_win,
            w_qkv[:, features + low : features + low + head_dim],
            preferred_element_type=jnp.float32,
        ).astype(jnp.bfloat16)
        value_part = jnp.dot(
            normed_win,
            w_qkv[:, 2 * features + low : 2 * features + low + head_dim],
            preferred_element_type=jnp.float32,
        ).astype(jnp.bfloat16)
        term = head_attention(
            query_part, key_part, value_part, allowed, w_out[low : low + head_dim]
        )
        mixed_win = term if mixed_win is None else mixed_win + term
    mixed = jnp.roll(merge_windows(mixed_win, levels, lat_rows, lon_cols), 1, axis=0)
    back_rows = shifted_2(mixed[:, -3:], "lat", 1)
    mixed = jnp.concatenate([back_rows, mixed[:, :-3]], axis=1)
    back_cols = shifted_2(mixed[:, :, -6:], "lon", 1)
    mixed = jnp.concatenate([back_cols, mixed[:, :, :-6]], axis=2)
    residual = (
        tokens.reshape(-1, features).astype(jnp.float32) + mixed.reshape(-1, features)
    ).astype(jnp.bfloat16)
    normed_mlp = layer_norm(residual, gain_mlp).astype(jnp.bfloat16)
    hidden = jax.nn.gelu(jnp.dot(normed_mlp, w_up, preferred_element_type=jnp.float32)).astype(
        jnp.bfloat16
    )
    block_out = residual.astype(jnp.float32) + jnp.dot(
        hidden, w_down, preferred_element_type=jnp.float32
    )
    return block_out.astype(jnp.bfloat16).reshape(tokens.shape)


def solution(mesh):
    in_specs = (P(None, "lat", "lon", None), P(), P(), P(), P(), P(), P())
    out_specs = P(None, "lat", "lon", None)
    return jax.shard_map(body, mesh=mesh, in_specs=in_specs, out_specs=out_specs, check_vma=False)
```

profile of v0, /device:TPU:2, one launch (start us, length us, event | category | flops | bytes accessed | tf_op | source)
XLA Modules:
  0.0 93.9 jit_solution(1357538621023238081)
XLA Ops:
  1.2 5.3 %collective-permute-start = (bf16[4,6,6,512]{3,0,2,1:T(4,128)(2,1)S(1)}, bf16[4,6,6,512]{3,0,2,1:T(4,128)(2,1)S(1)}, u32[]{:S(2)}, u32[]{:S(2)}) collective-permute-start(bf16[4,6,6,512]{3,0,2,1:T(4,128)(2,1)S(1)} %get-tuple-element.14), channel_id=1, source_target_pairs={{0,248},{8,0},{16,8},{24,16},{32,24},{40,32},{48,40},{56,48},{64,5... | collective-permute-start | bytes 442376 | tf_op jit(solution)/shard_map/ppermute | solution.py:12
  6.6 2.7 %collective-permute-done = bf16[4,6,6,512]{3,0,2,1:T(4,128)(2,1)S(1)} collective-permute-done((bf16[4,6,6,512]{3,0,2,1:T(4,128)(2,1)S(1)}, bf16[4,6,6,512]{3,0,2,1:T(4,128)(2,1)S(1)}, u32[]{:S(2)}, u32[]{:S(2)}) %collective-permute-start) | collective-permute-done | bytes 147488 | tf_op jit(solution)/shard_map/ppermute | solution.py:12
  9.5 4.9 %collective-permute-start.1 = (bf16[4,3,12,512]{3,0,2,1:T(4,128)(2,1)S(1)}, bf16[4,3,12,512]{3,0,2,1:T(4,128)(2,1)S(1)}, u32[]{:S(2)}, u32[]{:S(2)}) collective-permute-start(bf16[4,3,12,512]{3,0,2,1:T(4,128)(2,1)S(1)} %get-tuple-element.12), channel_id=1, source_target_pairs={{0,7},{1,0},{2,1},{3,2},{4,3},{5,4},{6,5},{7,6},{8,15},{9,8},{10,9... | collective-permute-start | bytes 442376 | tf_op jit(solution)/shard_map/ppermute | solution.py:12
  14.8 2.3 %collective-permute-done.1 = bf16[4,3,12,512]{3,0,2,1:T(4,128)(2,1)S(1)} collective-permute-done((bf16[4,3,12,512]{3,0,2,1:T(4,128)(2,1)S(1)}, bf16[4,3,12,512]{3,0,2,1:T(4,128)(2,1)S(1)}, u32[]{:S(2)}, u32[]{:S(2)}) %collective-permute-start.1) | collective-permute-done | bytes 147488 | tf_op jit(solution)/shard_map/ppermute | solution.py:12
  19.0 1.9 %convolution_convert_fusion.21 = bf16[2,144,64]{1,2,0:T(8,128)(2,1)} fusion(bf16[2,144,512]{2,1,0:T(8,128)(2,1)S(1)} %multiply_convert_fusion.1, bf16[512,1536]{1,0:T(8,128)(2,1)} %param.9), kind=kOutput, calls=%fused_computation.82 | convolution fusion | flops 18892800 | bytes 462848 | tf_op jit(solution)/shard_map/dot_general | solution.py:102
  29.3 2.0 %fusion.36 = f32[2,144,144]{1,2,0:T(8,128)} fusion(bf16[2,144,64]{1,2,0:T(8,128)(2,1)S(1)} %convolution_convert_fusion.22, bf16[2,144,512]{2,1,0:T(8,128)(2,1)S(1)} %multiply_convert_fusion.1, bf16[512,1536]{1,0:T(8,128)(2,1)} %param.9, f32[2,144]{1,0:T(2,128)S(1)} %broadcast_in_dim_broadcast_in_dim_broadcast_in_dim.17, ...), kind=kOutput, calls=%fused_computation.52 | convolution fusion | flops 24408576 | bytes 665600 | tf_op jit(solution)/shard_map/wqd,wkd->wqk/dot_general | solution.py:54
  31.3 1.7 %fusion.187 = f32[2,144]{1,0:T(2,128)} fusion(f32[2,144,144]{1,2,0:T(8,128)} %fusion.36), kind=kOutput, calls=%fused_computation.233 | output fusion | flops 83087 | bytes 167040 | tf_op jit(solution)/shard_map/sub | solution.py:59
  33.0 1.4 %fusion.35 = f32[2,144,144]{1,2,0:T(8,128)S(1)} fusion(bf16[2,144,64]{1,2,0:T(8,128)(2,1)S(1)} %convolution_convert_fusion.19, bf16[2,144,512]{2,1,0:T(8,128)(2,1)S(1)} %multiply_convert_fusion.1, bf16[512,1536]{1,0:T(8,128)(2,1)} %param.9, f32[2,144]{1,0:T(2,128)S(1)} %broadcast_in_dim_broadcast_in_dim_broadcast_in_dim.17, ...), kind=kOutput, calls=%fused_computation.50 | convolution fusion | flops 24408576 | bytes 665600 | tf_op jit(solution)/shard_map/wqd,wkd->wqk/dot_general | solution.py:54
  38.6 1.4 %fusion.33 = f32[2,144,144]{1,2,0:T(8,128)S(1)} fusion(bf16[2,144,64]{1,2,0:T(8,128)(2,1)S(1)} %convolution_convert_fusion.13, bf16[2,144,512]{2,1,0:T(8,128)(2,1)S(1)} %multiply_convert_fusion.1, bf16[512,1536]{1,0:T(8,128)(2,1)} %param.9, f32[2,144]{1,0:T(2,128)S(1)} %broadcast_in_dim_broadcast_in_dim_broadcast_in_dim.17, ...), kind=kOutput, calls=%fused_computation.46 | convolution fusion | flops 24408576 | bytes 665600 | tf_op jit(solution)/shard_map/wqd,wkd->wqk/dot_general | solution.py:54
  40.8 1.3 %fusion.32 = f32[2,144,144]{1,2,0:T(8,128)S(1)} fusion(bf16[2,144,64]{1,2,0:T(8,128)(2,1)S(1)} %convolution_convert_fusion.10, bf16[2,144,512]{2,1,0:T(8,128)(2,1)S(1)} %multiply_convert_fusion.1, bf16[512,1536]{1,0:T(8,128)(2,1)} %param.9, f32[2,144]{1,0:T(2,128)S(1)} %broadcast_in_dim_broadcast_in_dim_broadcast_in_dim.17, ...), kind=kOutput, calls=%fused_computation.44 | convolution fusion | flops 24408576 | bytes 665600 | tf_op jit(solution)/shard_map/wqd,wkd->wqk/dot_general | solution.py:54
  42.2 1.4 %fusion.31 = f32[2,144,144]{1,2,0:T(8,128)S(1)} fusion(bf16[2,144,64]{1,2,0:T(8,128)(2,1)S(1)} %convolution_convert_fusion.7, bf16[2,144,512]{2,1,0:T(8,128)(2,1)S(1)} %multiply_convert_fusion.1, bf16[512,1536]{1,0:T(8,128)(2,1)} %param.9, f32[2,144]{1,0:T(2,128)S(1)} %broadcast_in_dim_broadcast_in_dim_broadcast_in_dim.17, f32[2,144]{1,0:T(2,128)} %copy-done.13), kind=kOutput, calls=%fused_computation.42 | convolution fusion | flops 24408576 | bytes 665600 | tf_op jit(solution)/shard_map/wqd,wkd->wqk/dot_general | solution.py:54
  43.8 1.4 %fusion.30 = f32[2,144,144]{1,2,0:T(8,128)S(1)} fusion(bf16[2,144,64]{1,2,0:T(8,128)(2,1)} %convolution_convert_fusion.4, bf16[2,144,512]{2,1,0:T(8,128)(2,1)S(1)} %multiply_convert_fusion.1, bf16[512,1536]{1,0:T(8,128)(2,1)} %param.9, f32[2,144]{1,0:T(2,128)} %copy-done.12, f32[2,144]{1,0:T(2,128)} %copy-done.13), kind=kOutput, calls=%fused_computation.40 | convolution fusion | flops 24408576 | bytes 665600 | tf_op jit(solution)/shard_map/wqd,wkd->wqk/dot_general | solution.py:54
  45.2 1.4 %fusion.29 = f32[2,144,144]{1,2,0:T(8,128)S(1)} fusion(bf16[2,144,64]{1,2,0:T(8,128)(2,1)} %convolution_convert_fusion.1, bf16[2,144,512]{2,1,0:T(8,128)(2,1)S(1)} %multiply_convert_fusion.1, bf16[512,1536]{1,0:T(8,128)(2,1)} %param.9, f32[2,144]{1,0:T(2,128)} %copy-done.12, f32[2,144]{1,0:T(2,128)} %copy-done.13), kind=kOutput, calls=%fused_computation.38 | convolution fusion | flops 24408576 | bytes 665600 | tf_op jit(solution)/shard_map/wqd,wkd->wqk/dot_general | solution.py:54
  46.8 2.3 %fusion.45 = f32[2,144,512]{2,1,0:T(8,128)} fusion(bf16[2,144,64]{1,2,0:T(8,128)(2,1)} %convolution_convert_fusion.21, f32[2,144]{1,0:T(2,128)} %fusion.187, bf16[512,512]{1,0:T(8,128)(2,1)} %param.10, f32[2,144,144]{1,2,0:T(8,128)} %fusion.36), kind=kOutput, calls=%fused_computation.93 | convolution fusion | flops 24326064 | bytes 1312768 | tf_op jit(solution)/shard_map/dot_general | solution.py:64
  49.2 2.6 %convolution_add_fusion.6 = f32[2,144,512]{2,1,0:T(8,128)} fusion(f32[2,144,512]{2,1,0:T(8,128)} %fusion.45, bf16[2,144,64]{1,2,0:T(8,128)(2,1)S(1)} %copy-done.9, f32[2,144]{1,0:T(2,128)} %fusion.188, bf16[512,512]{1,0:T(8,128)(2,1)} %param.10, f32[2,144,144]{1,2,0:T(8,128)} %copy-done.6), kind=kOutput, calls=%fused_computation.23 | convolution fusion | flops 24473520 | bytes 1873920 | tf_op jit(solution)/shard_map/dot_general | solution.py:64
  51.7 2.5 %convolution_add_fusion.5 = f32[2,144,512]{2,1,0:T(8,128)} fusion(f32[2,144,512]{2,1,0:T(8,128)} %convolution_add_fusion.6, bf16[2,144,64]{1,2,0:T(8,128)(2,1)S(1)} %copy-done.8, f32[2,144]{1,0:T(2,128)S(1)} %copy-done.11, bf16[512,512]{1,0:T(8,128)(2,1)} %param.10, f32[2,144,144]{1,2,0:T(8,128)} %copy-done.5), kind=kOutput, calls=%fused_computation.22 | convolution fusion | flops 24473520 | bytes 1873024 | tf_op jit(solution)/shard_map/dot_general | solution.py:64
  54.3 2.5 %convolution_add_fusion.4 = f32[2,144,512]{2,1,0:T(8,128)} fusion(f32[2,144,512]{2,1,0:T(8,128)} %convolution_add_fusion.5, bf16[2,144,64]{1,2,0:T(8,128)(2,1)S(1)} %copy-done.7, f32[2,144]{1,0:T(2,128)S(1)} %fusion.190, bf16[512,512]{1,0:T(8,128)(2,1)} %param.10, f32[2,144,144]{1,2,0:T(8,128)} %copy-done.4), kind=kOutput, calls=%fused_computation.21 | convolution fusion | flops 24473520 | bytes 1873024 | tf_op jit(solution)/shard_map/dot_general | solution.py:64
  56.8 2.5 %convolution_add_fusion.3 = f32[2,144,512]{2,1,0:T(8,128)} fusion(f32[2,144,512]{2,1,0:T(8,128)} %convolution_add_fusion.4, bf16[2,144,64]{1,2,0:T(8,128)(2,1)S(1)} %convolution_convert_fusion.9, f32[2,144]{1,0:T(2,128)S(1)} %fusion.191, bf16[512,512]{1,0:T(8,128)(2,1)} %param.10, f32[2,144,144]{1,2,0:T(8,128)} %copy-done.3), kind=kOutput, calls=%fused_computation.20 | convolution fusion | flops 24473520 | bytes 1873024 | tf_op jit(solution)/shard_map/dot_general | solution.py:64
  59.3 2.3 %convolution_add_fusion.2 = f32[2,144,512]{2,1,0:T(8,128)} fusion(f32[2,144,512]{2,1,0:T(8,128)} %convolution_add_fusion.3, bf16[2,144,64]{1,2,0:T(8,128)(2,1)S(1)} %convolution_convert_fusion.6, f32[2,144]{1,0:T(2,128)S(1)} %fusion.192, bf16[512,512]{1,0:T(8,128)(2,1)} %param.10, f32[2,144,144]{1,2,0:T(8,128)S(1)} %fusion.31), kind=kOutput, calls=%fused_computation.19 | convolution fusion | flops 24473520 | bytes 1902592 | tf_op jit(solution)/shard_map/dot_general | solution.py:64
  61.7 2.3 %convolution_add_fusion.1 = f32[2,144,512]{2,1,0:T(8,128)} fusion(f32[2,144,512]{2,1,0:T(8,128)} %convolution_add_fusion.2, bf16[2,144,64]{1,2,0:T(8,128)(2,1)S(1)} %convolution_convert_fusion.3, f32[2,144]{1,0:T(2,128)S(1)} %fusion.193, bf16[512,512]{1,0:T(8,128)(2,1)} %param.10, f32[2,144,144]{1,2,0:T(8,128)S(1)} %fusion.30), kind=kOutput, calls=%fused_computation.18 | convolution fusion | flops 24473520 | bytes 1902592 | tf_op jit(solution)/shard_map/dot_general | solution.py:64
  64.0 1.5 %convolution_add_fusion = f32[2,144,512]{2,1,0:T(8,128)S(1)} fusion(f32[2,144,512]{2,1,0:T(8,128)} %convolution_add_fusion.1, bf16[2,144,64]{1,2,0:T(8,128)(2,1)S(1)} %convolution_convert_fusion, f32[2,144]{1,0:T(2,128)S(1)} %fusion.194, bf16[512,512]{1,0:T(8,128)(2,1)} %param.10, f32[2,144,144]{1,2,0:T(8,128)S(1)} %fusion.29), kind=kOutput, calls=%fused_computation.17 | convolution fusion | flops 24473520 | bytes 1902592 | tf_op jit(solution)/shard_map/dot_general | solution.py:64
  65.8 11.8 %collective-permute-done.2 = f32[4,3,12,512]{3,2,1,0:T(8,128)S(1)} collective-permute-done((f32[4,3,12,512]{3,2,1,0:T(8,128)S(1)}, f32[4,3,12,512]{3,2,1,0:T(8,128)S(1)}, u32[]{:S(2)}, u32[]{:S(2)}) %collective-permute-start.2) | collective-permute-done | bytes 294944 | tf_op jit(solution)/shard_map/ppermute | solution.py:12
  77.9 10.7 %collective-permute-done.3 = f32[4,6,6,512]{3,2,1,0:T(8,128)S(1)} collective-permute-done((f32[4,6,6,512]{3,2,1,0:T(8,128)S(1)}, f32[4,6,6,512]{3,2,1,0:T(8,128)S(1)}, u32[]{:S(2)}, u32[]{:S(2)}) %collective-permute-start.3) | collective-permute-done | bytes 294944 | tf_op jit(solution)/shard_map/ppermute | solution.py:12
  89.5 3.3 %fusion.16 = bf16[288,512]{1,0:T(8,128)(2,1)S(1)} fusion(f32[288,512]{1,0:T(8,128)S(1)} %reshape.103, bf16[2048,512]{1,0:T(8,128)(2,1)S(1)} %copy-done, bf16[512,2048]{1,0:T(8,128)(2,1)} %param.12, f32[512]{0:T(512)S(1)} %copy-done.14, f32[288]{0:T(512)S(1)} %rsqrt.25, f32[288]{0:T(512)S(1)} %div.120), kind=kOutput, calls=%fused_computation.25 | convolution fusion | flops 1214152704 | bytes 5083392 | tf_op jit(solution)/shard_map/dot_general | solution.py:123
  (90 shorter events, 19.6 us)
Async XLA Ops:
  0.0 89.4 %copy-start = (bf16[2048,512]{1,0:T(8,128)(2,1)S(1)}, bf16[2048,512]{1,0:T(8,128)(2,1)}, u32[]{:S(2)}) copy-start(bf16[2048,512]{1,0:T(8,128)(2,1)} %param.13) | copy-start | bytes 6291460
  1.2 8.0 %collective-permute-start = (bf16[4,6,6,512]{3,0,2,1:T(4,128)(2,1)S(1)}, bf16[4,6,6,512]{3,0,2,1:T(4,128)(2,1)S(1)}, u32[]{:S(2)}, u32[]{:S(2)}) collective-permute-start(bf16[4,6,6,512]{3,0,2,1:T(4,128)(2,1)S(1)} %get-tuple-element.14), channel_id=1, source_target_pairs={{0,248},{8,0},{16,8},{24,16},{32,24},{40,32},{48,40},{56,48},{64,5... | collective-permute-start | bytes 442376 | tf_op jit(solution)/shard_map/ppermute | solution.py:12
  9.5 7.6 %collective-permute-start.1 = (bf16[4,3,12,512]{3,0,2,1:T(4,128)(2,1)S(1)}, bf16[4,3,12,512]{3,0,2,1:T(4,128)(2,1)S(1)}, u32[]{:S(2)}, u32[]{:S(2)}) collective-permute-start(bf16[4,3,12,512]{3,0,2,1:T(4,128)(2,1)S(1)} %get-tuple-element.12), channel_id=1, source_target_pairs={{0,7},{1,0},{2,1},{3,2},{4,3},{5,4},{6,5},{7,6},{8,15},{9,8},{10,9... | collective-permute-start | bytes 442376 | tf_op jit(solution)/shard_map/ppermute | solution.py:12
  14.6 27.6 %copy-start.12 = (f32[2,144]{1,0:T(2,128)}, f32[2,144]{1,0:T(2,128)S(1)}, u32[]{:S(2)}) copy-start(f32[2,144]{1,0:T(2,128)S(1)} %broadcast_in_dim_broadcast_in_dim_broadcast_in_dim.17) | copy-start | bytes 3460
  14.8 26.0 %copy-start.13 = (f32[2,144]{1,0:T(2,128)}, f32[2,144]{1,0:T(2,128)S(1)}, u32[]{:S(2)}) copy-start(f32[2,144]{1,0:T(2,128)S(1)} %broadcast_in_dim_broadcast_in_dim_broadcast_in_dim.15) | copy-start | bytes 3460
  17.8 1.1 %copy-start.10 = (f32[512]{0:T(512)S(1)}, f32[512]{0:T(512)}, u32[]{:S(2)}) copy-start(f32[512]{0:T(512)} %param.8) | copy-start | bytes 6148
  18.8 3.2 %copy-start.1 = (bf16[512,1536]{1,0:T(8,128)(2,1)S(1)}, bf16[512,1536]{1,0:T(8,128)(2,1)}, u32[]{:S(2)}) copy-start(bf16[512,1536]{1,0:T(8,128)(2,1)} %param.9) | copy-start | bytes 4718596
  34.4 0.7 copy-start.6
  37.2 0.7 copy-start.5
  40.0 0.7 copy-start.4
  42.1 3.0 %copy-start.3 = (f32[2,144,144]{1,2,0:T(8,128)}, f32[2,144,144]{1,2,0:T(8,128)S(1)}, u32[]{:S(2)}) copy-start(f32[2,144,144]{1,2,0:T(8,128)S(1)} %fusion.32) | copy-start | bytes 497668
  46.7 2.5 %copy-start.9 = (bf16[2,144,64]{1,2,0:T(8,128)(2,1)S(1)}, bf16[2,144,64]{1,2,0:T(8,128)(2,1)}, u32[]{:S(2)}) copy-start(bf16[2,144,64]{1,2,0:T(8,128)(2,1)} %convolution_convert_fusion.18) | copy-start | bytes 110596
  46.8 4.9 %copy-start.8 = (bf16[2,144,64]{1,2,0:T(8,128)(2,1)S(1)}, bf16[2,144,64]{1,2,0:T(8,128)(2,1)}, u32[]{:S(2)}) copy-start(bf16[2,144,64]{1,2,0:T(8,128)(2,1)} %convolution_convert_fusion.15) | copy-start | bytes 110596
  46.8 4.9 %copy-start.11 = (f32[2,144]{1,0:T(2,128)S(1)}, f32[2,144]{1,0:T(2,128)}, u32[]{:S(2)}) copy-start(f32[2,144]{1,0:T(2,128)} %fusion.189) | copy-start | bytes 3460
  49.2 5.1 %copy-start.7 = (bf16[2,144,64]{1,2,0:T(8,128)(2,1)S(1)}, bf16[2,144,64]{1,2,0:T(8,128)(2,1)}, u32[]{:S(2)}) copy-start(bf16[2,144,64]{1,2,0:T(8,128)(2,1)} %convolution_convert_fusion.12) | copy-start | bytes 110596
  65.7 22.9 %copy-start.2 = (bf16[4,6,12,512]{3,0,2,1:T(4,128)(2,1)S(1)}, bf16[4,6,12,512]{3,0,2,1:T(4,128)(2,1)}, u32[]{:S(2)}) copy-start(bf16[4,6,12,512]{3,0,2,1:T(4,128)(2,1)} %param.7) | copy-start | bytes 884740
  65.7 11.9 %collective-permute-start.2 = (f32[4,3,12,512]{3,2,1,0:T(8,128)S(1)}, f32[4,3,12,512]{3,2,1,0:T(8,128)S(1)}, u32[]{:S(2)}, u32[]{:S(2)}) collective-permute-start(f32[4,3,12,512]{3,2,1,0:T(8,128)S(1)} %fusion.49), channel_id=1, source_target_pairs={{0,1},{1,2},{2,3},{3,4},{4,5},{5,6},{6,7},{7,0},{8,9},{9,10},{10,1... | collective-permute-start | bytes 884744 | tf_op jit(solution)/shard_map/ppermute | solution.py:12
  77.8 10.8 %collective-permute-start.3 = (f32[4,6,6,512]{3,2,1,0:T(8,128)S(1)}, f32[4,6,6,512]{3,2,1,0:T(8,128)S(1)}, u32[]{:S(2)}, u32[]{:S(2)}) collective-permute-start(f32[4,6,6,512]{3,2,1,0:T(8,128)S(1)} %get-tuple-element.9), channel_id=1, source_target_pairs={{0,8},{8,16},{16,24},{24,32},{32,40},{40,48},{48,56},{56,64},{64,7... | collective-permute-start | bytes 884744 | tf_op jit(solution)/shard_map/ppermute | solution.py:12
  88.9 0.7 copy-start.14
where the time goes:
time: 94.4 us; the launch traced here: 93.9 us
  matrix products  43.8 us (46%)
  waiting for transfers between devices  27.5 us (29%)
  starting transfers between devices  10.5 us (11%)
  local copies, waits for them, and re-layouts  6 us (6%)
  other arithmetic  5.61 us (6%)
    ppermute x4, waiting for transfers between devices, shifted_2(): return lax.ppermute(value, axis, pairs)  27.5 us
    dot_general x8, matrix products, head_attention(): return jnp.dot(attended, w_out_rows, preferred_element_type=jnp.float32)  18.7 us
    dot_general x8, matrix products, head_attention(): jnp.einsum('wqd,wkd->wqk', query_part, key_part, preferred_element_type=j...  11.7 us
    ppermute x4, starting transfers between devices, shifted_2(): return lax.ppermute(value, axis, pairs)  10.5 us
    dot_general x8, matrix products, body(): jnp.dot(normed_win, w_qkv[:, 2 * features + low:2 * features + low + head...  5.75 us
    dot_general x8, matrix products, body(): jnp.dot(normed_win, w_qkv[:, features + low:features + low + head_dim], p...  4.4 us
    sub x8, other arithmetic, head_attention(): raised = jnp.exp(scores - ceiling)  3.61 us
    dot_general x1, matrix products, body(): jnp.dot(hidden, w_down, preferred_element_type=jnp.float32)  3.28 us
  transfers between devices with their start and end apart: 4, of which 4 were waited for; matrix products, arithmetic and copies ran while one was open for 0% of the time, Pallas kernels for 0%

commit v1 on v0

v1 whole, which is shorter than its diff:
```python
import functools

import jax
import jax.numpy as jnp
from jax import lax
from jax.experimental import pallas as pl
from jax.experimental.pallas import tpu as pltpu
from jax.sharding import PartitionSpec as P

HEADS = 8
D = 512
FF = 2048
HEAD_DIM = 64
F32 = jnp.float32
BF16 = jnp.bfloat16
MESH = pl.DeviceIdType.MESH


def norm(values, gain):
    average = jnp.mean(values, axis=-1, keepdims=True)
    centered = values - average
    spread = jnp.mean(centered * centered, axis=-1, keepdims=True)
    return (centered * lax.rsqrt(spread + 1e-05) * gain).astype(BF16)


def flat(block):
    rows = block.shape[0] * block.shape[1] * block.shape[2]
    return block.reshape(rows, block.shape[3])


def gelu(v):
    inner = v * (0.7978845608028654 + 0.035677408136300125 * (v * v))
    return (0.5 * v) * (1.0 + jnp.tanh(inner))


def dot(a, b):
    return jnp.dot(a, b, preferred_element_type=F32)


def dot_t(a, b):
    return lax.dot_general(a, b, (((1,), (1,)), ((), ())), preferred_element_type=F32)


def kernel(
    n_lat,
    n_lon,
    x_hbm,
    gain_attn,
    w_qkv_hbm,
    w_out_hbm,
    gain_mlp,
    w_up_hbm,
    w_down_hbm,
    o_ref,
    xv,
    halo,
    back,
    got,
    bias,
    w_qkv,
    w_out,
    w_up,
    w_down,
    send_sem,
    recv_sem,
    back_send,
    back_recv,
    w_sem,
    x_sem,
):
    lat = lax.axis_index("lat")
    lon = lax.axis_index("lon")
    west = lax.rem(lon + n_lon - 1, n_lon)
    east = lax.rem(lon + 1, n_lon)
    has_north = lat > 0
    has_south = lat < n_lat - 1

    barrier = pltpu.get_barrier_semaphore()

    def greet(la, lo):
        pl.semaphore_signal(barrier, inc=1, device_id={"lat": la, "lon": lo}, device_id_type=MESH)

    greet(lat, west)

    @pl.when(has_north)
    def _():
        greet(lat - 1, lon)
        greet(lat - 1, west)

    @pl.when(has_south)
    def _():
        greet(lat + 1, lon)
        greet(lat + 1, west)

    loads = [
        pltpu.make_async_copy(x_hbm, xv, x_sem.at[0]),
        pltpu.make_async_copy(x_hbm.at[:, 0:6], halo.at[3:9, 6:12], x_sem.at[1]),
        pltpu.make_async_copy(w_qkv_hbm, w_qkv, w_sem.at[0]),
        pltpu.make_async_copy(w_out_hbm, w_out, w_sem.at[1]),
        pltpu.make_async_copy(w_up_hbm, w_up, w_sem.at[2]),
        pltpu.make_async_copy(w_down_hbm, w_down, w_sem.at[3]),
    ]
    for load in loads:
        load.start()

    def send(index, src, dst, la, lo):
        return pltpu.make_async_remote_copy(
            src_ref=src,
            dst_ref=dst,
            send_sem=send_sem.at[index],
            recv_sem=recv_sem.at[index],
            device_id={"lat": la, "lon": lo},
            device_id_type=MESH,
        )

    to_east = send(0, x_hbm.at[:, 6:12], halo.at[3:9, 0:6], lat, east)
    to_north = [
        send(1, x_hbm.at[0:3, 0:6], halo.at[9:12, 6:12], lat - 1, lon),
        send(2, x_hbm.at[0:3, 6:12], halo.at[9:12, 0:6], lat - 1, east),
    ]
    to_south = [
        send(3, x_hbm.at[3:6, 0:6], halo.at[0:3, 6:12], lat + 1, lon),
        send(4, x_hbm.at[3:6, 6:12], halo.at[0:3, 0:6], lat + 1, east),
    ]

    pl.semaphore_wait(barrier, 1 + 2 * (has_north.astype(jnp.int32) + has_south.astype(jnp.int32)))
    to_east.start()

    @pl.when(has_north)
    def _():
        for copy in to_north:
            copy.start()

    @pl.when(has_south)
    def _():
        for copy in to_south:
            copy.start()

    key = lax.broadcasted_iota(jnp.int32, (144, 288), 1)
    query = lax.broadcasted_iota(jnp.int32, (144, 288), 0)
    same = lax.div(lax.rem(key, 4) + 1, 2) == lax.div(lax.rem(query, 4) + 1, 2)
    bias[0] = jnp.where(same & ((key >= 144) | has_north), 0.0, -1e30)
    bias[1] = jnp.where(same & ((key < 144) | has_south), 0.0, -1e30)

    @pl.when(jnp.logical_not(has_north))
    def _():
        halo[0:3] = jnp.zeros((3, 12, 4, D), BF16)

    @pl.when(jnp.logical_not(has_south))
    def _():
        halo[9:12] = jnp.zeros((3, 12, 4, D), BF16)

    loads[0].wait()
    loads[1].wait()
    loads[2].wait()
    to_east.wait_recv()

    def give_back(band):
        return pltpu.make_async_remote_copy(
            src_ref=back.at[band],
            dst_ref=got.at[band],
            send_sem=back_send.at[band],
            recv_sem=back_recv.at[band],
            device_id={"lat": lat, "lon": west},
            device_id_type=MESH,
        )

    lane = lax.broadcasted_iota(jnp.int32, (1, 128), 1)
    low = lane < HEAD_DIM
    mine = []
    for band in range(2):
        present, copies = ((has_north, to_south), (has_south, to_north))[band]

        @pl.when(present)
        def _():
            for copy in copies:
                copy.wait_recv()

        normed = norm(flat(halo[6 * band : 6 * band + 6]).astype(F32), gain_attn[...])
        normed_q = normed[144:288] if band == 0 else normed[0:144]
        q = (dot(normed_q, w_qkv[:, 0:D]) * HEAD_DIM**-0.5).astype(BF16)
        k = dot(normed, w_qkv[:, D : 2 * D]).astype(BF16)
        v = dot(normed, w_qkv[:, 2 * D : 3 * D]).astype(BF16)
        parts = []
        for pair in range(HEADS // 2):
            cols = slice(128 * pair, 128 * pair + 128)
            q_pair, k_pair, v_pair = q[:, cols], k[:, cols], v[:, cols]
            outs = []
            for first in (True, False):
                keep = low if first else jnp.logical_not(low)
                scores = dot_t(q_pair, jnp.where(keep, k_pair, jnp.zeros_like(k_pair))) + bias[band]
                raised = jnp.exp(scores - jnp.max(scores, axis=-1, keepdims=True))
                total = jnp.sum(raised, axis=-1, keepdims=True)
                weights = (raised * (1.0 / total)).astype(BF16)
                outs.append(dot(weights, v_pair))
            parts.append(jnp.where(low, outs[0], outs[1]))
        attended = jnp.concatenate(parts, axis=1).astype(BF16).reshape(3, 12, 4, D)
        back[band] = attended[:, 0:6]
        give_back(band).start()
        mine.append(flat(attended[:, 6:12]))

    loads[3].wait()
    loads[4].wait()
    loads[5].wait()
    for half in range(2):
        if half == 0:
            attended = jnp.concatenate(mine, axis=0)
        else:
            give_back(0).wait_recv()
            give_back(1).wait_recv()
            attended = jnp.concatenate([flat(got[0]), flat(got[1])], axis=0)
        cols = slice(6 * half, 6 * half + 6)
        residual = (flat(xv[:, cols]).astype(F32) + dot(attended, w_out[...])).astype(BF16).astype(F32)
        hidden = gelu(dot(norm(residual, gain_mlp[...]), w_up[...])).astype(BF16)
        block = (residual + dot(hidden, w_down[...])).astype(BF16)
        o_ref[:, cols] = block.reshape(6, 6, 4, D)

    to_east.wait_send()

    @pl.when(has_north)
    def _():
        for copy in to_north:
            copy.wait_send()

    @pl.when(has_south)
    def _():
        for copy in to_south:
            copy.wait_send()

    give_back(0).wait_send()
    give_back(1).wait_send()


def solution(mesh):
    n_lat, n_lon = mesh.shape["lat"], mesh.shape["lon"]

    def body(tokens, gain_attn, w_qkv, w_out, gain_mlp, w_up, w_down):
        x = tokens.transpose(1, 2, 0, 3)
        hbm = pl.BlockSpec(memory_space=pltpu.HBM)
        vmem = pl.BlockSpec(memory_space=pltpu.VMEM)
        out = pl.pallas_call(
            functools.partial(kernel, n_lat, n_lon),
            out_shape=jax.ShapeDtypeStruct(x.shape, BF16),
            in_specs=[hbm, vmem, hbm, hbm, vmem, hbm, hbm],
            out_specs=vmem,
            scratch_shapes=[
                pltpu.VMEM((6, 12, 4, D), BF16),
                pltpu.VMEM((12, 12, 4, D), BF16),
                pltpu.VMEM((2, 3, 6, 4, D), BF16),
                pltpu.VMEM((2, 3, 6, 4, D), BF16),
                pltpu.VMEM((2, 144, 288), F32),
                pltpu.VMEM((D, 3 * D), BF16),
                pltpu.VMEM((D, D), BF16),
                pltpu.VMEM((D, FF), BF16),
                pltpu.VMEM((FF, D), BF16),
                pltpu.SemaphoreType.DMA((5,)),
                pltpu.SemaphoreType.DMA((5,)),
                pltpu.SemaphoreType.DMA((2,)),
                pltpu.SemaphoreType.DMA((2,)),
                pltpu.SemaphoreType.DMA((4,)),
                pltpu.SemaphoreType.DMA((2,)),
            ],
            compiler_params=pltpu.CompilerParams(
                collective_id=0, has_side_effects=True, vmem_limit_bytes=58 * 1024 * 1024
            ),
            cost_estimate=pl.CostEstimate(flops=2_500_000_000, bytes_accessed=7_000_000, transcendentals=1_500_000),
        )(x, gain_attn.reshape(1, D), w_qkv, w_out, gain_mlp.reshape(1, D), w_up, w_down)
        return out.transpose(2, 0, 1, 3)

    in_specs = (P(None, "lat", "lon", None), P(), P(), P(), P(), P(), P())
    out_specs = P(None, "lat", "lon", None)
    return jax.shard_map(body, mesh=mesh, in_specs=in_specs, out_specs=out_specs, check_vma=False)
```

time: 94.4 us -> 29.5 us (0.31)
  the two profiles are of different devices: /device:TPU:2 before, /device:TPU:103 now
where the time goes in v1:
time: 29.5 us; the launch traced here: 29.3 us
  Pallas kernels  27.6 us (94%)
  local copies, waits for them, and re-layouts  1.78 us (6%)
    pallas_call x1, Pallas kernels, body(): pl.pallas_call(functools.partial(kernel, n_lat, n_lon), out_shape=jax.Sha...  27.6 us
    unnamed x1, local copies, waits for them, and re-layouts  1.78 us

profile of v1, /device:TPU:103, one launch (start us, length us, event | category | flops | bytes accessed | tf_op | source)
XLA Modules:
  0.0 29.3 jit_solution(16079438579925308784)
XLA Ops:
  0.0 27.6 %shard_map.73 = bf16[6,12,4,512]{3,2,1,0:T(4,128)(2,1)} custom-call(bf16[6,12,4,512]{3,2,1,0:T(4,128)(2,1)} %bitcast.5, f32[1,512]{1,0:T(1,128)} %bitcast.6, bf16[512,1536]{1,0:T(8,128)(2,1)} %w_qkv_hbm.1, bf16[512,512]{1,0:T(8,128)(2,1)} %w_out_hbm.1, f32[1,512]{1,0:T(1,128)} %bitcast.7, bf16[512,2048]{1,0:T(8,128)(2,1)} %w_up_hbm.1, ...), custom_call_target="tpu_custom_call" | custom-call | flops 2500000000 | bytes 7000000 | tf_op jit(solution)/shard_map/pallas_call | solution.py:241
  27.6 1.8 %copy.9 = bf16[4,6,12,512]{3,0,2,1:T(4,128)(2,1)} copy(bf16[4,6,12,512]{3,0,2,1:T(4,128)(2,1)} %bitcast.4) | data formatting | bytes 589824

commit v2 on v1

--- a/solution.py
+++ b/solution.py
@@ -16,11 +16,36 @@
 MESH = pl.DeviceIdType.MESH
 
 
-def norm(values, gain):
+def norm32(values, gain):
     average = jnp.mean(values, axis=-1, keepdims=True)
     centered = values - average
     spread = jnp.mean(centered * centered, axis=-1, keepdims=True)
-    return (centered * lax.rsqrt(spread + 1e-05) * gain).astype(BF16)
+    return centered * lax.rsqrt(spread + 1e-05) * gain
+
+
+def norm(values, gain):
+    return norm32(values, gain).astype(BF16)
+
+
+def inner_levels(shape):
+    place = lax.rem(lax.broadcasted_iota(jnp.int32, shape, 1), 4)
+    return (place == 1) | (place == 2)
+
+
+def split_levels(values):
+    pairs = values.reshape(values.shape[0] // 16, 2, 8, values.shape[1])
+    first, second = pairs[:, 0], pltpu.roll(pairs[:, 1], 2, 1)
+    inner = inner_levels(first.shape)
+    half = (values.shape[0] // 2, values.shape[1])
+    return jnp.where(inner, first, second).reshape(half), jnp.where(inner, second, first).reshape(half)
+
+
+def join_levels(inner_half, outer_half):
+    shape = (inner_half.shape[0] // 8, 8, inner_half.shape[1])
+    a, b = inner_half.reshape(shape), outer_half.reshape(shape)
+    inner = inner_levels(shape)
+    first, second = jnp.where(inner, a, b), pltpu.roll(jnp.where(inner, b, a), 6, 1)
+    return jnp.stack([first, second], axis=1).reshape(2 * inner_half.shape[0], inner_half.shape[1])
 
 
 def flat(block):
@@ -56,6 +81,7 @@
     halo,
     back,
     got,
+    mine,
     bias,
     w_qkv,
     w_out,
@@ -136,11 +162,12 @@
         for copy in to_south:
             copy.start()
 
-    key = lax.broadcasted_iota(jnp.int32, (144, 288), 1)
-    query = lax.broadcasted_iota(jnp.int32, (144, 288), 0)
-    same = lax.div(lax.rem(key, 4) + 1, 2) == lax.div(lax.rem(query, 4) + 1, 2)
-    bias[0] = jnp.where(same & ((key >= 144) | has_north), 0.0, -1e30)
-    bias[1] = jnp.where(same & ((key < 144) | has_south), 0.0, -1e30)
+    key = lax.broadcasted_iota(jnp.int32, (288, 144), 1)
+    query = lax.broadcasted_iota(jnp.int32, (288, 144), 0)
+    same = lax.rem(key + query, 2) == 0
+    for band, known in enumerate(((key >= 72) | has_north, (key < 72) | has_south)):
+        bias[band, 0] = jnp.where(known, 0.0, -1e30)
+        bias[band, 1] = jnp.where(known & same, 0.0, -1e30)
 
     @pl.when(jnp.logical_not(has_north))
     def _():
@@ -165,46 +192,56 @@
             device_id_type=MESH,
         )
 
-    lane = lax.broadcasted_iota(jnp.int32, (1, 128), 1)
-    low = lane < HEAD_DIM
-    mine = []
-    for band in range(2):
-        present, copies = ((has_north, to_south), (has_south, to_north))[band]
-
-        @pl.when(present)
+    head = lax.div(lax.broadcasted_iota(jnp.int32, (72, 256), 1), HEAD_DIM)
+    first = (lat >= n_lat // 2).astype(jnp.int32)
+    for step in range(2):
+        band = first if step == 0 else 1 - first
+
+        @pl.when((band == 0) & has_north)
         def _():
-            for copy in copies:
+            for copy in to_south:
                 copy.wait_recv()
 
-        normed = norm(flat(halo[6 * band : 6 * band + 6]).astype(F32), gain_attn[...])
-        normed_q = normed[144:288] if band == 0 else normed[0:144]
-        q = (dot(normed_q, w_qkv[:, 0:D]) * HEAD_DIM**-0.5).astype(BF16)
-        k = dot(normed, w_qkv[:, D : 2 * D]).astype(BF16)
-        v = dot(normed, w_qkv[:, 2 * D : 3 * D]).astype(BF16)
-        parts = []
-        for pair in range(HEADS // 2):
-            cols = slice(128 * pair, 128 * pair + 128)
-            q_pair, k_pair, v_pair = q[:, cols], k[:, cols], v[:, cols]
-            outs = []
-            for first in (True, False):
-                keep = low if first else jnp.logical_not(low)
-                scores = dot_t(q_pair, jnp.where(keep, k_pair, jnp.zeros_like(k_pair))) + bias[band]
+        @pl.when((band == 1) & has_south)
+        def _():
+            for copy in to_north:
+                copy.wait_recv()
+
+        normed = split_levels(norm32(flat(halo[pl.ds(6 * band, 6)]).astype(F32), gain_attn[...]))
+        mixed = []
+        for group in range(2):
+            tokens = normed[group].astype(BF16)
+            own = jnp.where(band == 0, normed[group][72:144], normed[group][0:72]).astype(BF16)
+            q = (dot(own, w_qkv[:, 0:D]) * HEAD_DIM**-0.5).astype(BF16)
+            k = dot(tokens, w_qkv[:, D : 2 * D]).astype(BF16)
+            v = dot(tokens, w_qkv[:, 2 * D : 3 * D]).astype(BF16)
+            parts = []
+            for quad in range(2):
+                cols = slice(256 * quad, 256 * quad + 256)
+                q_quad = q[:, cols]
+                zero = jnp.zeros_like(q_quad)
+                stacked = jnp.concatenate([jnp.where(head == h, q_quad, zero) for h in range(4)], axis=0)
+                scores = dot_t(stacked, k[:, cols]) + bias[band, group]
                 raised = jnp.exp(scores - jnp.max(scores, axis=-1, keepdims=True))
                 total = jnp.sum(raised, axis=-1, keepdims=True)
                 weights = (raised * (1.0 / total)).astype(BF16)
-                outs.append(dot(weights, v_pair))
-            parts.append(jnp.where(low, outs[0], outs[1]))
-        attended = jnp.concatenate(parts, axis=1).astype(BF16).reshape(3, 12, 4, D)
+                out = dot(weights, v[:, cols])
+                part = out[0:72]
+                for h in range(1, 4):
+                    part = jnp.where(head == h, out[72 * h : 72 * h + 72], part)
+                parts.append(part)
+            mixed.append(jnp.concatenate(parts, axis=1))
+        attended = join_levels(*mixed).astype(BF16).reshape(3, 12, 4, D)
         back[band] = attended[:, 0:6]
         give_back(band).start()
-        mine.append(flat(attended[:, 6:12]))
+        mine[band] = attended[:, 6:12]
 
     loads[3].wait()
     loads[4].wait()
     loads[5].wait()
     for half in range(2):
         if half == 0:
-            attended = jnp.concatenate(mine, axis=0)
+            attended = jnp.concatenate([flat(mine[0]), flat(mine[1])], axis=0)
         else:
             give_back(0).wait_recv()
             give_back(1).wait_recv()
@@ -248,7 +285,8 @@
                 pltpu.VMEM((12, 12, 4, D), BF16),
                 pltpu.VMEM((2, 3, 6, 4, D), BF16),
                 pltpu.VMEM((2, 3, 6, 4, D), BF16),
-                pltpu.VMEM((2, 144, 288), F32),
+                pltpu.VMEM((2, 3, 6, 4, D), BF16),
+                pltpu.VMEM((2, 2, 288, 144), F32),
                 pltpu.VMEM((D, 3 * D), BF16),
                 pltpu.VMEM((D, D), BF16),
                 pltpu.VMEM((D, FF), BF16),

time: 29.5 us -> 24.2 us (0.82)
  Pallas kernels: 27.6 us -> 22.3 us
    pallas_call x1, Pallas kernels: 27.6 us -> 22.3 us  [body(): pl.pallas_call(functools.partial(kernel, n_lat, n_lon), out_shape=jax.Sha...]
where the time goes in v2:
time: 24.2 us; the launch traced here: 24.1 us
  Pallas kernels  22.3 us (92%)
  local copies, waits for them, and re-layouts  1.78 us (7%)
    pallas_call x1, Pallas kernels, body(): pl.pallas_call(functools.partial(kernel, n_lat, n_lon), out_shape=jax.Sha...  22.3 us
    unnamed x1, local copies, waits for them, and re-layouts  1.78 us

profile of v2, /device:TPU:103, one launch (start us, length us, event | category | flops | bytes accessed | tf_op | source)
XLA Modules:
  0.0 24.1 jit_solution(825658354990941367)
XLA Ops:
  0.0 22.3 %shard_map.73 = bf16[6,12,4,512]{3,2,1,0:T(4,128)(2,1)} custom-call(bf16[6,12,4,512]{3,2,1,0:T(4,128)(2,1)} %bitcast.5, f32[1,512]{1,0:T(1,128)} %bitcast.6, bf16[512,1536]{1,0:T(8,128)(2,1)} %w_qkv_hbm.1, bf16[512,512]{1,0:T(8,128)(2,1)} %w_out_hbm.1, f32[1,512]{1,0:T(1,128)} %bitcast.7, bf16[512,2048]{1,0:T(8,128)(2,1)} %w_up_hbm.1, ...), custom_call_target="tpu_custom_call" | custom-call | flops 2500000000 | bytes 7000000 | tf_op jit(solution)/shard_map/pallas_call | solution.py:278
  22.3 1.8 %copy.9 = bf16[4,6,12,512]{3,0,2,1:T(4,128)(2,1)} copy(bf16[4,6,12,512]{3,0,2,1:T(4,128)(2,1)} %bitcast.4) | data formatting | bytes 589824

commit v3 on v2

--- a/solution.py
+++ b/solution.py
@@ -66,33 +66,54 @@
     return lax.dot_general(a, b, (((1,), (1,)), ((), ())), preferred_element_type=F32)
 
 
+def feed_forward(attended, x, w_out, gain, w_up, w_down):
+    residual = (flat(x).astype(F32) + dot(attended, w_out[...])).astype(BF16).astype(F32)
+    hidden = gelu(dot(norm(residual, gain[...]), w_up[...])).astype(BF16)
+    block = (residual + dot(hidden, w_down[...])).astype(BF16)
+    return block.reshape(x.shape)
+
+
+def finish(early, late, xv, w_out, gain, w_up, w_down, o_hbm, done, sem):
+    put = pltpu.make_async_copy(early, o_hbm.at[:, 0:6], sem.at[0])
+    put.start()
+    done[...] = feed_forward(flat(late[...]), xv[:, 6:12], w_out, gain, w_up, w_down)
+    last = pltpu.make_async_copy(done, o_hbm.at[:, 6:12], sem.at[1])
+    last.start()
+    put.wait()
+    last.wait()
+
+
 def kernel(
     n_lat,
     n_lon,
     x_hbm,
-    gain_attn,
+    gain_attn_hbm,
     w_qkv_hbm,
     w_out_hbm,
-    gain_mlp,
+    gain_mlp_hbm,
     w_up_hbm,
     w_down_hbm,
-    o_ref,
+    early,
+    late,
     xv,
+    w_out,
+    gain_mlp,
+    w_up,
+    w_down,
+    gain_attn,
     halo,
     back,
     got,
     mine,
     bias,
     w_qkv,
-    w_out,
-    w_up,
-    w_down,
     send_sem,
     recv_sem,
     back_send,
     back_recv,
     w_sem,
     x_sem,
+    ok_sem,
 ):
     lat = lax.axis_index("lat")
     lon = lax.axis_index("lon")
@@ -106,22 +127,29 @@
     def greet(la, lo):
         pl.semaphore_signal(barrier, inc=1, device_id={"lat": la, "lon": lo}, device_id_type=MESH)
 
+    middle = n_lat // 2
+
+    def at_once(sender_lon, far):
+        return far | (lax.rem(sender_lon, 2) == 0) | (lax.rem(sender_lon, n_lon // 2) == n_lon // 2 - 1)
+
+    far_north, far_south = lat == middle, lat == middle - 1
     greet(lat, west)
-
-    @pl.when(has_north)
-    def _():
-        greet(lat - 1, lon)
-        greet(lat - 1, west)
-
-    @pl.when(has_south)
-    def _():
-        greet(lat + 1, lon)
-        greet(lat + 1, west)
+    for present, far, other in ((has_north, far_north, lat - 1), (has_south, far_south, lat + 1)):
+
+        @pl.when(present)
+        def _():
+            greet(other, lon)
+
+        @pl.when(present & at_once(west, far))
+        def _():
+            greet(other, west)
 
     loads = [
         pltpu.make_async_copy(x_hbm, xv, x_sem.at[0]),
         pltpu.make_async_copy(x_hbm.at[:, 0:6], halo.at[3:9, 6:12], x_sem.at[1]),
+        pltpu.make_async_copy(gain_attn_hbm, gain_attn, w_sem.at[4]),
         pltpu.make_async_copy(w_qkv_hbm, w_qkv, w_sem.at[0]),
+        pltpu.make_async_copy(gain_mlp_hbm, gain_mlp, w_sem.at[5]),
         pltpu.make_async_copy(w_out_hbm, w_out, w_sem.at[1]),
         pltpu.make_async_copy(w_up_hbm, w_up, w_sem.at[2]),
         pltpu.make_async_copy(w_down_hbm, w_down, w_sem.at[3]),
@@ -149,18 +177,34 @@
         send(4, x_hbm.at[3:6, 6:12], halo.at[0:3, 0:6], lat + 1, east),
     ]
 
-    pl.semaphore_wait(barrier, 1 + 2 * (has_north.astype(jnp.int32) + has_south.astype(jnp.int32)))
+    ways = ((has_north, far_north, lat - 1, 0, to_north), (has_south, far_south, lat + 1, 1, to_south))
+    greetings = 1
+    for present, far, _, _, _ in ways:
+        greetings += present.astype(jnp.int32) + (present & at_once(lon, far)).astype(jnp.int32)
+    pl.semaphore_wait(barrier, greetings)
     to_east.start()
-
-    @pl.when(has_north)
-    def _():
-        for copy in to_north:
-            copy.start()
-
-    @pl.when(has_south)
-    def _():
-        for copy in to_south:
-            copy.start()
+    for present, far, other, way, copies in ways:
+
+        @pl.when(present)
+        def _():
+            copies[0].start()
+
+        @pl.when(present & jnp.logical_not(at_once(lon, far)))
+        def _():
+            pl.semaphore_signal(
+                ok_sem.at[1 - way], inc=1, device_id={"lat": other, "lon": lon}, device_id_type=MESH
+            )
+
+        @pl.when(present & at_once(lon, far))
+        def _():
+            copies[1].start()
+
+    for present, far, other, way, copies in ways:
+
+        @pl.when(present & jnp.logical_not(at_once(lon, far)))
+        def _():
+            pl.semaphore_wait(ok_sem.at[way], 1)
+            copies[1].start()
 
     key = lax.broadcasted_iota(jnp.int32, (288, 144), 1)
     query = lax.broadcasted_iota(jnp.int32, (288, 144), 0)
@@ -176,11 +220,6 @@
     @pl.when(jnp.logical_not(has_south))
     def _():
         halo[9:12] = jnp.zeros((3, 12, 4, D), BF16)
-
-    loads[0].wait()
-    loads[1].wait()
-    loads[2].wait()
-    to_east.wait_recv()
 
     def give_back(band):
         return pltpu.make_async_remote_copy(
@@ -191,6 +230,13 @@
             device_id={"lat": lat, "lon": west},
             device_id_type=MESH,
         )
+
+    loads[0].wait()
+    loads[1].wait()
+    loads[2].wait()
+    loads[3].wait()
+
+    to_east.wait_recv()
 
     head = lax.div(lax.broadcasted_iota(jnp.int32, (72, 256), 1), HEAD_DIM)
     first = (lat >= n_lat // 2).astype(jnp.int32)
@@ -236,21 +282,14 @@
         give_back(band).start()
         mine[band] = attended[:, 6:12]
 
-    loads[3].wait()
-    loads[4].wait()
-    loads[5].wait()
-    for half in range(2):
-        if half == 0:
-            attended = jnp.concatenate([flat(mine[0]), flat(mine[1])], axis=0)
-        else:
-            give_back(0).wait_recv()
-            give_back(1).wait_recv()
-            attended = jnp.concatenate([flat(got[0]), flat(got[1])], axis=0)
-        cols = slice(6 * half, 6 * half + 6)
-        residual = (flat(xv[:, cols]).astype(F32) + dot(attended, w_out[...])).astype(BF16).astype(F32)
-        hidden = gelu(dot(norm(residual, gain_mlp[...]), w_up[...])).astype(BF16)
-        block = (residual + dot(hidden, w_down[...])).astype(BF16)
-        o_ref[:, cols] = block.reshape(6, 6, 4, D)
+    for load in loads[4:]:
+        load.wait()
+    early[...] = feed_forward(
+        jnp.concatenate([flat(mine[0]), flat(mine[1])], axis=0), xv[:, 0:6], w_out, gain_mlp, w_up, w_down
+    )
+    for band in range(2):
+        give_back(band).wait_recv()
+        late[3 * band : 3 * band + 3] = got[band]
 
     to_east.wait_send()
 
@@ -273,36 +312,50 @@
 
     def body(tokens, gain_attn, w_qkv, w_out, gain_mlp, w_up, w_down):
         x = tokens.transpose(1, 2, 0, 3)
+        gain_attn, gain_mlp = gain_attn.reshape(1, D), gain_mlp.reshape(1, D)
         hbm = pl.BlockSpec(memory_space=pltpu.HBM)
         vmem = pl.BlockSpec(memory_space=pltpu.VMEM)
-        out = pl.pallas_call(
+        held = [
+            pltpu.with_memory_space_constraint(a, pltpu.HBM)
+            for a in (x, gain_attn, w_qkv, w_out, gain_mlp, w_up, w_down)
+        ]
+        half = jax.ShapeDtypeStruct((6, 6, 4, D), BF16)
+        passed = [jax.ShapeDtypeStruct(a.shape, a.dtype) for a in (x, w_out, gain_mlp, w_up, w_down)]
+        made = pl.pallas_call(
             functools.partial(kernel, n_lat, n_lon),
-            out_shape=jax.ShapeDtypeStruct(x.shape, BF16),
-            in_specs=[hbm, vmem, hbm, hbm, vmem, hbm, hbm],
-            out_specs=vmem,
+            out_shape=[half, half] + passed,
+            in_specs=[hbm] * 7,
+            out_specs=[vmem] * 7,
             scratch_shapes=[
-                pltpu.VMEM((6, 12, 4, D), BF16),
+                pltpu.VMEM((1, D), F32),
                 pltpu.VMEM((12, 12, 4, D), BF16),
                 pltpu.VMEM((2, 3, 6, 4, D), BF16),
                 pltpu.VMEM((2, 3, 6, 4, D), BF16),
                 pltpu.VMEM((2, 3, 6, 4, D), BF16),
                 pltpu.VMEM((2, 2, 288, 144), F32),
                 pltpu.VMEM((D, 3 * D), BF16),
-                pltpu.VMEM((D, D), BF16),
-                pltpu.VMEM((D, FF), BF16),
-                pltpu.VMEM((FF, D), BF16),
                 pltpu.SemaphoreType.DMA((5,)),
                 pltpu.SemaphoreType.DMA((5,)),
                 pltpu.SemaphoreType.DMA((2,)),
                 pltpu.SemaphoreType.DMA((2,)),
-                pltpu.SemaphoreType.DMA((4,)),
+                pltpu.SemaphoreType.DMA((6,)),
                 pltpu.SemaphoreType.DMA((2,)),
+                pltpu.SemaphoreType.REGULAR((2,)),
             ],
             compiler_params=pltpu.CompilerParams(
-                collective_id=0, has_side_effects=True, vmem_limit_bytes=58 * 1024 * 1024
+                collective_id=0, has_side_effects=True, vmem_limit_bytes=40 * 1024 * 1024
             ),
-            cost_estimate=pl.CostEstimate(flops=2_500_000_000, bytes_accessed=7_000_000, transcendentals=1_500_000),
-        )(x, gain_attn.reshape(1, D), w_qkv, w_out, gain_mlp.reshape(1, D), w_up, w_down)
+            cost_estimate=pl.CostEstimate(flops=1_800_000_000, bytes_accessed=7_000_000, transcendentals=1_000_000),
+        )(*held)
+        out = pl.pallas_call(
+            finish,
+            out_shape=jax.ShapeDtypeStruct(x.shape, BF16),
+            in_specs=[vmem] * 7,
+            out_specs=hbm,
+            scratch_shapes=[pltpu.VMEM((6, 6, 4, D), BF16), pltpu.SemaphoreType.DMA((2,))],
+            compiler_params=pltpu.CompilerParams(vmem_limit_bytes=40 * 1024 * 1024),
+            cost_estimate=pl.CostEstimate(flops=700_000_000, bytes_accessed=300_000, transcendentals=300_000),
+        )(*made)
         return out.transpose(2, 0, 1, 3)
 
     in_specs = (P(None, "lat", "lon", None), P(), P(), P(), P(), P(), P())

time: 24.2 us -> 21.3 us (0.88)
  local copies, waits for them, and re-layouts: 1.78 us -> 0 us
  Pallas kernels: 22.3 us -> 21.2 us
    unnamed x1 -> x0, local copies, waits for them, and re-layouts: 1.78 us -> none
    pallas_call x1 -> x2, Pallas kernels: 22.3 us -> 21.2 us  [the longest x1 19.1 us: body(): pl.pallas_call(functools.partial(kernel, n_lat, n_lon), out_shape=[half,...]
where the time goes in v3:
time: 21.3 us; the launch traced here: 21.2 us
  Pallas kernels  21.2 us (100%)
    pallas_call x1, Pallas kernels, body(): pl.pallas_call(functools.partial(kernel, n_lat, n_lon), out_shape=[half,...  19.1 us
    pallas_call x1, Pallas kernels, body(): pl.pallas_call(finish, out_shape=jax.ShapeDtypeStruct(x.shape, BF16), in_...  2.06 us

profile of v3, /device:TPU:103, one launch (start us, length us, event | category | flops | bytes accessed | tf_op | source)
XLA Modules:
  0.0 21.2 jit_solution(6081161761882056772)
XLA Ops:
  0.0 19.1 %shard_map.73 = (bf16[6,6,4,512]{3,2,1,0:T(4,128)(2,1)S(1)}, bf16[6,6,4,512]{3,2,1,0:T(4,128)(2,1)S(1)}, bf16[6,12,4,512]{3,2,1,0:T(4,128)(2,1)S(1)}, bf16[512,5...) custom-call(bf16[6,12,4,512]{3,2,1,0:T(4,128)(2,1)} %bitcast.4, ...), custom_call_target="tpu_custom_call" | custom-call | flops 1800000000 | bytes 7000000 | tf_op jit(solution)/shard_map/pallas_call | solution.py:324
  19.1 2.1 %shard_map.74 = bf16[6,12,4,512]{3,2,1,0:T(4,128)(2,1)} custom-call(bf16[6,6,4,512]{3,2,1,0:T(4,128)(2,1)S(1)} %get-tuple-element.12.early, bf16[6,6,4,512]{3,2,1,0:T(4,128)(2,1)S(1)} %get-tuple-element.13.late, bf16[6,12,4,512]{3,2,1,0:T(4,128)(2,1)S(1)} %get-tuple-element.14.xv, bf16[512,512]{1,0:T(8,128)(2,1)S(1)} %get-tuple-element.15.w_out, ...), custom_call_target="tpu_custom_call" | custom-call | flops 700000000 | bytes 300000 | tf_op jit(solution)/shard_map/pallas_call | solution.py:350

commit v4 on v3

--- a/solution.py
+++ b/solution.py
@@ -102,9 +102,9 @@
     w_down,
     gain_attn,
     halo,
-    back,
+    made,
+    own,
     got,
-    mine,
     bias,
     w_qkv,
     send_sem,
@@ -133,20 +133,32 @@
         return far | (lax.rem(sender_lon, 2) == 0) | (lax.rem(sender_lon, n_lon // 2) == n_lon // 2 - 1)
 
     far_north, far_south = lat == middle, lat == middle - 1
+    even = lax.rem(lon, 2) == 0
+    seven, eight = lax.rem(lon, n_lon // 2) == n_lon // 4 - 1, lax.rem(lon, n_lon // 2) == n_lon // 4
     greet(lat, west)
+
+    @pl.when(seven)
+    def _():
+        greet(lat, east)
+
     for present, far, other in ((has_north, far_north, lat - 1), (has_south, far_south, lat + 1)):
 
-        @pl.when(present)
+        @pl.when(present & even)
         def _():
             greet(other, lon)
 
         @pl.when(present & at_once(west, far))
         def _():
             greet(other, west)
+
+        @pl.when(present & seven)
+        def _():
+            greet(other, east)
 
     loads = [
         pltpu.make_async_copy(x_hbm, xv, x_sem.at[0]),
-        pltpu.make_async_copy(x_hbm.at[:, 0:6], halo.at[3:9, 6:12], x_sem.at[1]),
+        pltpu.make_async_copy(x_hbm.at[:, 0:6], halo.at[0, 3:9, 6:12], x_sem.at[1]),
+        pltpu.make_async_copy(x_hbm.at[:, 6:12], halo.at[1, 3:9, 0:6], x_sem.at[2]),
         pltpu.make_async_copy(gain_attn_hbm, gain_attn, w_sem.at[4]),
         pltpu.make_async_copy(w_qkv_hbm, w_qkv, w_sem.at[0]),
         pltpu.make_async_copy(gain_mlp_hbm, gain_mlp, w_sem.at[5]),
@@ -167,27 +179,68 @@
             device_id_type=MESH,
         )
 
-    to_east = send(0, x_hbm.at[:, 6:12], halo.at[3:9, 0:6], lat, east)
+    to_east = send(0, x_hbm.at[:, 6:12], halo.at[0, 3:9, 0:6], lat, east)
     to_north = [
-        send(1, x_hbm.at[0:3, 0:6], halo.at[9:12, 6:12], lat - 1, lon),
-        send(2, x_hbm.at[0:3, 6:12], halo.at[9:12, 0:6], lat - 1, east),
+        send(1, x_hbm.at[0:3, 0:6], halo.at[0, 9:12, 6:12], lat - 1, lon),
+        send(2, x_hbm.at[0:3, 6:12], halo.at[0, 9:12, 0:6], lat - 1, east),
     ]
     to_south = [
-        send(3, x_hbm.at[3:6, 0:6], halo.at[0:3, 6:12], lat + 1, lon),
-        send(4, x_hbm.at[3:6, 6:12], halo.at[0:3, 0:6], lat + 1, east),
+        send(3, x_hbm.at[3:6, 0:6], halo.at[0, 0:3, 6:12], lat + 1, lon),
+        send(4, x_hbm.at[3:6, 6:12], halo.at[0, 0:3, 0:6], lat + 1, east),
     ]
-
-    ways = ((has_north, far_north, lat - 1, 0, to_north), (has_south, far_south, lat + 1, 1, to_south))
-    greetings = 1
-    for present, far, _, _, _ in ways:
-        greetings += present.astype(jnp.int32) + (present & at_once(lon, far)).astype(jnp.int32)
+    to_west = send(5, x_hbm.at[:, 0:6], halo.at[1, 3:9, 6:12], lat, west)
+    to_north_2 = [
+        send(6, x_hbm.at[0:3, 6:12], halo.at[1, 9:12, 0:6], lat - 1, lon),
+        send(7, x_hbm.at[0:3, 0:6], halo.at[1, 9:12, 6:12], lat - 1, west),
+    ]
+    to_south_2 = [
+        send(8, x_hbm.at[3:6, 6:12], halo.at[1, 0:3, 0:6], lat + 1, lon),
+        send(9, x_hbm.at[3:6, 0:6], halo.at[1, 0:3, 6:12], lat + 1, west),
+    ]
+
+    ways = (
+        (has_north, far_north, lat - 1, 0, to_north, to_north_2),
+        (has_south, far_south, lat + 1, 1, to_south, to_south_2),
+    )
+    greetings = 1 + eight.astype(jnp.int32)
+    for present, far, *_ in ways:
+        for greets in (even, at_once(lon, far), eight):
+            greetings += (present & greets).astype(jnp.int32)
     pl.semaphore_wait(barrier, greetings)
+
+    @pl.when(even)
+    def _():
+        pl.semaphore_signal(ok_sem.at[2], inc=1, device_id={"lat": lat, "lon": east}, device_id_type=MESH)
+
     to_east.start()
-    for present, far, other, way, copies in ways:
+
+    @pl.when(eight)
+    def _():
+        to_west.start()
+
+    for present, far, other, way, copies, copies_2 in ways:
+
+        @pl.when(present & at_once(lon, far))
+        def _():
+            copies[1].start()
+
+        @pl.when(present & eight)
+        def _():
+            copies_2[1].start()
+
+    @pl.when(jnp.logical_not(even))
+    def _():
+        pl.semaphore_wait(ok_sem.at[2], 1)
+
+    for present, far, other, way, copies, copies_2 in ways:
 
         @pl.when(present)
         def _():
             copies[0].start()
+
+        @pl.when(present & seven)
+        def _():
+            copies_2[0].start()
 
         @pl.when(present & jnp.logical_not(at_once(lon, far)))
         def _():
@@ -195,11 +248,7 @@
                 ok_sem.at[1 - way], inc=1, device_id={"lat": other, "lon": lon}, device_id_type=MESH
             )
 
-        @pl.when(present & at_once(lon, far))
-        def _():
-            copies[1].start()
-
-    for present, far, other, way, copies in ways:
+    for present, far, other, way, copies, copies_2 in ways:
 
         @pl.when(present & jnp.logical_not(at_once(lon, far)))
         def _():
@@ -209,21 +258,21 @@
     key = lax.broadcasted_iota(jnp.int32, (288, 144), 1)
     query = lax.broadcasted_iota(jnp.int32, (288, 144), 0)
     same = lax.rem(key + query, 2) == 0
-    for band, known in enumerate(((key >= 72) | has_north, (key < 72) | has_south)):
+    for band, known in enumerate(((key >= 72) | has_north, (key >= 72) | has_south)):
         bias[band, 0] = jnp.where(known, 0.0, -1e30)
         bias[band, 1] = jnp.where(known & same, 0.0, -1e30)
 
     @pl.when(jnp.logical_not(has_north))
     def _():
-        halo[0:3] = jnp.zeros((3, 12, 4, D), BF16)
+        halo[:, 0:3] = jnp.zeros((2, 3, 12, 4, D), BF16)
 
     @pl.when(jnp.logical_not(has_south))
     def _():
-        halo[9:12] = jnp.zeros((3, 12, 4, D), BF16)
+        halo[:, 9:12] = jnp.zeros((2, 3, 12, 4, D), BF16)
 
     def give_back(band):
         return pltpu.make_async_remote_copy(
-            src_ref=back.at[band],
+            src_ref=made.at[0, band, :, 0:6],
             dst_ref=got.at[band],
             send_sem=back_send.at[band],
             recv_sem=back_recv.at[band],
@@ -231,36 +280,57 @@
             device_id_type=MESH,
         )
 
-    loads[0].wait()
-    loads[1].wait()
-    loads[2].wait()
-    loads[3].wait()
-
-    to_east.wait_recv()
+    for load in loads[:5]:
+        load.wait()
 
     head = lax.div(lax.broadcasted_iota(jnp.int32, (72, 256), 1), HEAD_DIM)
-    first = (lat >= n_lat // 2).astype(jnp.int32)
-    for step in range(2):
-        band = first if step == 0 else 1 - first
-
-        @pl.when((band == 0) & has_north)
-        def _():
-            for copy in to_south:
-                copy.wait_recv()
-
-        @pl.when((band == 1) & has_south)
-        def _():
-            for copy in to_north:
-                copy.wait_recv()
-
-        normed = split_levels(norm32(flat(halo[pl.ds(6 * band, 6)]).astype(F32), gain_attn[...]))
+    first = (lat >= middle).astype(jnp.int32)
+    windows = 1 + seven.astype(jnp.int32)
+
+    def project(block):
+        normed = norm32(flat(block).astype(F32), gain_attn[...])
+        return jnp.concatenate(split_levels(normed), axis=0).astype(BF16)
+
+    def own_rows(window):
+        @pl.when(window == 0)
+        def _():
+            to_east.wait_recv()
+
+        @pl.when(window == 1)
+        def _():
+            to_west.wait_recv()
+
+        tokens = project(halo[window, 3:9])
+        for group in range(2):
+            rows = tokens[144 * group : 144 * group + 144]
+            for part in range(3):
+                own[window, group, part] = dot(rows, w_qkv[:, D * part : D * part + D])
+
+    def step(index, carry):
+        window, turn = lax.rem(index, windows), lax.div(index, windows)
+        band = lax.rem(first + turn, 2)
+
+        @pl.when(turn == 0)
+        def _():
+            own_rows(window)
+
+        for side, way in ((0, 1), (1, 0)):
+            for which in range(2):
+
+                @pl.when((band == side) & ways[side][0] & (window == which))
+                def _():
+                    for copy in ways[way][4 + which]:
+                        copy.wait_recv()
+
+        tokens = project(halo[window, pl.ds(9 * band, 3)])
+        others = [dot(tokens, w_qkv[:, D * part : D * part + D]) for part in (1, 2)]
         mixed = []
         for group in range(2):
-            tokens = normed[group].astype(BF16)
-            own = jnp.where(band == 0, normed[group][72:144], normed[group][0:72]).astype(BF16)
-            q = (dot(own, w_qkv[:, 0:D]) * HEAD_DIM**-0.5).astype(BF16)
-            k = dot(tokens, w_qkv[:, D : 2 * D]).astype(BF16)
-            v = dot(tokens, w_qkv[:, 2 * D : 3 * D]).astype(BF16)
+            rows = slice(72 * group, 72 * group + 72)
+            q, k_own, v_own = [own[window, group, part, pl.ds(72 * band, 72)] for part in range(3)]
+            q = (q * HEAD_DIM**-0.5).astype(BF16)
+            k = jnp.concatenate([others[0][rows], k_own], axis=0).astype(BF16)
+            v = jnp.concatenate([others[1][rows], v_own], axis=0).astype(BF16)
             parts = []
             for quad in range(2):
                 cols = slice(256 * quad, 256 * quad + 256)
@@ -270,41 +340,64 @@
                 scores = dot_t(stacked, k[:, cols]) + bias[band, group]
                 raised = jnp.exp(scores - jnp.max(scores, axis=-1, keepdims=True))
                 total = jnp.sum(raised, axis=-1, keepdims=True)
-                weights = (raised * (1.0 / total)).astype(BF16)
-                out = dot(weights, v[:, cols])
+                out = dot(raised.astype(BF16), v[:, cols]) * (1.0 / total)
                 part = out[0:72]
                 for h in range(1, 4):
                     part = jnp.where(head == h, out[72 * h : 72 * h + 72], part)
                 parts.append(part)
             mixed.append(jnp.concatenate(parts, axis=1))
-        attended = join_levels(*mixed).astype(BF16).reshape(3, 12, 4, D)
-        back[band] = attended[:, 0:6]
-        give_back(band).start()
-        mine[band] = attended[:, 6:12]
-
-    for load in loads[4:]:
+        made[window, band] = join_levels(*mixed).astype(BF16).reshape(3, 12, 4, D)
+
+        @pl.when((window == 0) & jnp.logical_not(eight))
+        def _():
+            give_back(band).start()
+
+        return carry
+
+    lax.fori_loop(0, 2 * windows, step, 0)
+
+    for load in loads[5:]:
         load.wait()
     early[...] = feed_forward(
-        jnp.concatenate([flat(mine[0]), flat(mine[1])], axis=0), xv[:, 0:6], w_out, gain_mlp, w_up, w_down
+        jnp.concatenate([flat(made[0, 0, :, 6:12]), flat(made[0, 1, :, 6:12])], axis=0), xv[:, 0:6], w_out, gain_mlp, w_up, w_down
     )
-    for band in range(2):
-        give_back(band).wait_recv()
-        late[3 * band : 3 * band + 3] = got[band]
+
+    @pl.when(seven)
+    def _():
+        for band in range(2):
+            late[3 * band : 3 * band + 3] = made[1, band, :, 0:6]
+
+    @pl.when(jnp.logical_not(seven))
+    def _():
+        for band in range(2):
+            give_back(band).wait_recv()
+            late[3 * band : 3 * band + 3] = got[band]
 
     to_east.wait_send()
 
-    @pl.when(has_north)
-    def _():
-        for copy in to_north:
-            copy.wait_send()
-
-    @pl.when(has_south)
-    def _():
-        for copy in to_south:
-            copy.wait_send()
-
-    give_back(0).wait_send()
-    give_back(1).wait_send()
+    @pl.when(eight)
+    def _():
+        to_west.wait_send()
+
+    for present, _, _, _, copies, copies_2 in ways:
+
+        @pl.when(present)
+        def _():
+            for copy in copies:
+                copy.wait_send()
+
+        @pl.when(present & seven)
+        def _():
+            copies_2[0].wait_send()
+
+        @pl.when(present & eight)
+        def _():
+            copies_2[1].wait_send()
+
+    @pl.when(jnp.logical_not(eight))
+    def _():
+        give_back(0).wait_send()
+        give_back(1).wait_send()
 
 
 def solution(mesh):
@@ -328,19 +421,19 @@
             out_specs=[vmem] * 7,
             scratch_shapes=[
                 pltpu.VMEM((1, D), F32),
-                pltpu.VMEM((12, 12, 4, D), BF16),
-                pltpu.VMEM((2, 3, 6, 4, D), BF16),
-                pltpu.VMEM((2, 3, 6, 4, D), BF16),
+                pltpu.VMEM((2, 12, 12, 4, D), BF16),
+                pltpu.VMEM((2, 2, 3, 12, 4, D), BF16),
+                pltpu.VMEM((2, 2, 3, 144, D), F32),
                 pltpu.VMEM((2, 3, 6, 4, D), BF16),
                 pltpu.VMEM((2, 2, 288, 144), F32),
                 pltpu.VMEM((D, 3 * D), BF16),
-                pltpu.SemaphoreType.DMA((5,)),
-                pltpu.SemaphoreType.DMA((5,)),
+                pltpu.SemaphoreType.DMA((10,)),
+                pltpu.SemaphoreType.DMA((10,)),
                 pltpu.SemaphoreType.DMA((2,)),
                 pltpu.SemaphoreType.DMA((2,)),
                 pltpu.SemaphoreType.DMA((6,)),
-                pltpu.SemaphoreType.DMA((2,)),
-                pltpu.SemaphoreType.REGULAR((2,)),
+                pltpu.SemaphoreType.DMA((3,)),
+                pltpu.SemaphoreType.REGULAR((3,)),
             ],
             compiler_params=pltpu.CompilerParams(
                 collective_id=0, has_side_effects=True, vmem_limit_bytes=40 * 1024 * 1024

time: 21.3 us -> 18.4 us (0.86)
  Pallas kernels: 21.2 us -> 18.3 us
    pallas_call x1, Pallas kernels: 19.1 us -> 16.2 us  [body(): pl.pallas_call(functools.partial(kernel, n_lat, n_lon), out_shape=[half,...]
where the time goes in v4:
time: 18.4 us; the launch traced here: 18.3 us
  Pallas kernels  18.3 us (99%)
    pallas_call x1, Pallas kernels, body(): pl.pallas_call(functools.partial(kernel, n_lat, n_lon), out_shape=[half,...  16.2 us
    pallas_call x1, Pallas kernels, body(): pl.pallas_call(finish, out_shape=jax.ShapeDtypeStruct(x.shape, BF16), in_...  2.06 us

profile of v4, /device:TPU:103, one launch (start us, length us, event | category | flops | bytes accessed | tf_op | source)
XLA Modules:
  0.0 18.3 jit_solution(5619106960377522486)
XLA Ops:
  0.0 16.2 %shard_map.73 = (bf16[6,6,4,512]{3,2,1,0:T(4,128)(2,1)S(1)}, bf16[6,6,4,512]{3,2,1,0:T(4,128)(2,1)S(1)}, bf16[6,12,4,512]{3,2,1,0:T(4,128)(2,1)S(1)}, bf16[512,5...) custom-call(bf16[6,12,4,512]{3,2,1,0:T(4,128)(2,1)} %bitcast.4, ...), custom_call_target="tpu_custom_call" | custom-call | flops 1800000000 | bytes 7000000 | tf_op jit(solution)/shard_map/pallas_call | solution.py:417
  16.2 2.1 %shard_map.74 = bf16[6,12,4,512]{3,2,1,0:T(4,128)(2,1)} custom-call(bf16[6,6,4,512]{3,2,1,0:T(4,128)(2,1)S(1)} %get-tuple-element.12.early, bf16[6,6,4,512]{3,2,1,0:T(4,128)(2,1)S(1)} %get-tuple-element.13.late, bf16[6,12,4,512]{3,2,1,0:T(4,128)(2,1)S(1)} %get-tuple-element.14.xv, bf16[512,512]{1,0:T(8,128)(2,1)S(1)} %get-tuple-element.15.w_out, ...), custom_call_target="tpu_custom_call" | custom-call | flops 700000000 | bytes 300000 | tf_op jit(solution)/shard_map/pallas_call | solution.py:443

commit v5 on v4

--- a/solution.py
+++ b/solution.py
@@ -73,11 +73,12 @@
     return block.reshape(x.shape)
 
 
-def finish(early, late, xv, w_out, gain, w_up, w_down, o_hbm, done, sem):
-    put = pltpu.make_async_copy(early, o_hbm.at[:, 0:6], sem.at[0])
+def finish(n_lon, early, late, xv, w_out, gain, w_up, w_down, o_hbm, done, sem):
+    eastern = 6 * (lax.rem(lax.axis_index("lon"), n_lon // 2) == n_lon // 4 - 1).astype(jnp.int32)
+    put = pltpu.make_async_copy(early, o_hbm.at[:, pl.ds(eastern, 6)], sem.at[0])
     put.start()
-    done[...] = feed_forward(flat(late[...]), xv[:, 6:12], w_out, gain, w_up, w_down)
-    last = pltpu.make_async_copy(done, o_hbm.at[:, 6:12], sem.at[1])
+    done[...] = feed_forward(flat(late[...]), xv[:, pl.ds(6 - eastern, 6)], w_out, gain, w_up, w_down)
+    last = pltpu.make_async_copy(done, o_hbm.at[:, pl.ds(6 - eastern, 6)], sem.at[1])
     last.start()
     put.wait()
     last.wait()
@@ -128,30 +129,30 @@
         pl.semaphore_signal(barrier, inc=1, device_id={"lat": la, "lon": lo}, device_id_type=MESH)
 
     middle = n_lat // 2
-
-    def at_once(sender_lon, far):
-        return far | (lax.rem(sender_lon, 2) == 0) | (lax.rem(sender_lon, n_lon // 2) == n_lon // 2 - 1)
-
     far_north, far_south = lat == middle, lat == middle - 1
     even = lax.rem(lon, 2) == 0
-    seven, eight = lax.rem(lon, n_lon // 2) == n_lon // 4 - 1, lax.rem(lon, n_lon // 2) == n_lon // 4
+    place = lax.rem(lon, n_lon // 2)
+    first_place, last_place = place == 0, place == n_lon // 2 - 1
+    six, seven, eight = place == n_lon // 4 - 2, place == n_lon // 4 - 1, place == n_lon // 4
+    wider, pushes = six | seven, seven | eight
+    told = jnp.logical_not(even | last_place)
     greet(lat, west)
 
-    @pl.when(seven)
+    @pl.when(told | six)
     def _():
         greet(lat, east)
 
-    for present, far, other in ((has_north, far_north, lat - 1), (has_south, far_south, lat + 1)):
+    for present, other in ((has_north, lat - 1), (has_south, lat + 1)):
 
         @pl.when(present & even)
         def _():
             greet(other, lon)
 
-        @pl.when(present & at_once(west, far))
+        @pl.when(present & (jnp.logical_not(even) | first_place))
         def _():
             greet(other, west)
 
-        @pl.when(present & seven)
+        @pl.when(present & wider)
         def _():
             greet(other, east)
 
@@ -198,65 +199,84 @@
         send(9, x_hbm.at[3:6, 0:6], halo.at[1, 0:3, 6:12], lat + 1, west),
     ]
 
-    ways = (
-        (has_north, far_north, lat - 1, 0, to_north, to_north_2),
-        (has_south, far_south, lat + 1, 1, to_south, to_south_2),
-    )
-    greetings = 1 + eight.astype(jnp.int32)
-    for present, far, *_ in ways:
-        for greets in (even, at_once(lon, far), eight):
+    ways = ((has_north, far_north, to_north, to_north_2), (has_south, far_south, to_south, to_south_2))
+
+    def straight(far):
+        for present, is_far, copies, copies_2 in ways:
+
+            @pl.when(present & (is_far == far) & jnp.logical_not(seven))
+            def _():
+                copies[0].start()
+
+            @pl.when(present & wider & (is_far == far))
+            def _():
+                copies_2[0].start()
+
+    def corner(far):
+        for present, is_far, copies, copies_2 in ways:
+
+            @pl.when(present & (is_far == far) & jnp.logical_not(six))
+            def _():
+                copies[1].start()
+
+            @pl.when(present & pushes & (is_far == far))
+            def _():
+                copies_2[1].start()
+
+    greetings = 1 + ((even & jnp.logical_not(first_place)) | seven).astype(jnp.int32)
+    for present, *_ in ways:
+        for greets in (even, jnp.logical_not(told), pushes):
             greetings += (present & greets).astype(jnp.int32)
     pl.semaphore_wait(barrier, greetings)
 
     @pl.when(even)
     def _():
-        pl.semaphore_signal(ok_sem.at[2], inc=1, device_id={"lat": lat, "lon": east}, device_id_type=MESH)
-
-    to_east.start()
-
-    @pl.when(eight)
-    def _():
-        to_west.start()
-
-    for present, far, other, way, copies, copies_2 in ways:
-
-        @pl.when(present & at_once(lon, far))
-        def _():
-            copies[1].start()
-
-        @pl.when(present & eight)
-        def _():
-            copies_2[1].start()
-
-    @pl.when(jnp.logical_not(even))
-    def _():
-        pl.semaphore_wait(ok_sem.at[2], 1)
-
-    for present, far, other, way, copies, copies_2 in ways:
-
-        @pl.when(present)
-        def _():
-            copies[0].start()
-
-        @pl.when(present & seven)
-        def _():
-            copies_2[0].start()
-
-        @pl.when(present & jnp.logical_not(at_once(lon, far)))
-        def _():
-            pl.semaphore_signal(
-                ok_sem.at[1 - way], inc=1, device_id={"lat": other, "lon": lon}, device_id_type=MESH
-            )
-
-    for present, far, other, way, copies, copies_2 in ways:
-
-        @pl.when(present & jnp.logical_not(at_once(lon, far)))
-        def _():
-            pl.semaphore_wait(ok_sem.at[way], 1)
-            copies[1].start()
-
-    key = lax.broadcasted_iota(jnp.int32, (288, 144), 1)
-    query = lax.broadcasted_iota(jnp.int32, (288, 144), 0)
+        pl.semaphore_signal(ok_sem.at[0], inc=1, device_id={"lat": lat, "lon": east}, device_id_type=MESH)
+
+        @pl.when(jnp.logical_not(first_place))
+        def _():
+            pl.semaphore_signal(ok_sem.at[1], inc=1, device_id={"lat": lat, "lon": west}, device_id_type=MESH)
+
+        straight(True)
+        straight(False)
+
+        @pl.when(jnp.logical_not(six))
+        def _():
+            to_east.start()
+
+        @pl.when(eight)
+        def _():
+            to_west.start()
+
+        corner(True)
+        corner(False)
+
+    @pl.when(last_place)
+    def _():
+        to_east.start()
+        corner(True)
+        corner(False)
+        pl.semaphore_wait(ok_sem.at[0], 1)
+        straight(False)
+        straight(True)
+
+    @pl.when(told)
+    def _():
+        to_east.start()
+
+        @pl.when(seven)
+        def _():
+            to_west.start()
+
+        pl.semaphore_wait(ok_sem.at[0], 1)
+        straight(False)
+        pl.semaphore_wait(ok_sem.at[1], 1)
+        corner(True)
+        corner(False)
+        straight(True)
+
+    key = lax.broadcasted_iota(jnp.int32, (144, 144), 1)
+    query = lax.broadcasted_iota(jnp.int32, (144, 144), 0)
     same = lax.rem(key + query, 2) == 0
     for band, known in enumerate(((key >= 72) | has_north, (key >= 72) | has_south)):
         bias[band, 0] = jnp.where(known, 0.0, -1e30)
@@ -280,12 +300,23 @@
             device_id_type=MESH,
         )
 
+    def give_on(band):
+        return pltpu.make_async_remote_copy(
+            src_ref=made.at[1, band, :, 6:12],
+            dst_ref=got.at[band],
+            send_sem=back_send.at[2 + band],
+            recv_sem=back_recv.at[band],
+            device_id={"lat": lat, "lon": east},
+            device_id_type=MESH,
+        )
+
     for load in loads[:5]:
         load.wait()
 
-    head = lax.div(lax.broadcasted_iota(jnp.int32, (72, 256), 1), HEAD_DIM)
+    low = lax.broadcasted_iota(jnp.int32, (72, 128), 1) < HEAD_DIM
     first = (lat >= middle).astype(jnp.int32)
-    windows = 1 + seven.astype(jnp.int32)
+    only = seven.astype(jnp.int32)
+    middle_rows = far_north | far_south
 
     def project(block):
         normed = norm32(flat(block).astype(F32), gain_attn[...])
@@ -306,8 +337,7 @@
             for part in range(3):
                 own[window, group, part] = dot(rows, w_qkv[:, D * part : D * part + D])
 
-    def step(index, carry):
-        window, turn = lax.rem(index, windows), lax.div(index, windows)
+    def step(window, turn):
         band = lax.rem(first + turn, 2)
 
         @pl.when(turn == 0)
@@ -319,7 +349,7 @@
 
                 @pl.when((band == side) & ways[side][0] & (window == which))
                 def _():
-                    for copy in ways[way][4 + which]:
+                    for copy in ways[way][2 + which]:
                         copy.wait_recv()
 
         tokens = project(halo[window, pl.ds(9 * band, 3)])
@@ -332,19 +362,16 @@
             k = jnp.concatenate([others[0][rows], k_own], axis=0).astype(BF16)
             v = jnp.concatenate([others[1][rows], v_own], axis=0).astype(BF16)
             parts = []
-            for quad in range(2):
-                cols = slice(256 * quad, 256 * quad + 256)
-                q_quad = q[:, cols]
-                zero = jnp.zeros_like(q_quad)
-                stacked = jnp.concatenate([jnp.where(head == h, q_quad, zero) for h in range(4)], axis=0)
+            for pair in range(HEADS // 2):
+                cols = slice(128 * pair, 128 * pair + 128)
+                q_pair = q[:, cols]
+                zero = jnp.zeros_like(q_pair)
+                stacked = jnp.concatenate([jnp.where(low, q_pair, zero), jnp.where(low, zero, q_pair)], axis=0)
                 scores = dot_t(stacked, k[:, cols]) + bias[band, group]
                 raised = jnp.exp(scores - jnp.max(scores, axis=-1, keepdims=True))
                 total = jnp.sum(raised, axis=-1, keepdims=True)
                 out = dot(raised.astype(BF16), v[:, cols]) * (1.0 / total)
-                part = out[0:72]
-                for h in range(1, 4):
-                    part = jnp.where(head == h, out[72 * h : 72 * h + 72], part)
-                parts.append(part)
+                parts.append(jnp.where(low, out[0:72], out[72:144]))
             mixed.append(jnp.concatenate(parts, axis=1))
         made[window, band] = join_levels(*mixed).astype(BF16).reshape(3, 12, 4, D)
 
@@ -352,52 +379,60 @@
         def _():
             give_back(band).start()
 
-        return carry
-
-    lax.fori_loop(0, 2 * windows, step, 0)
+        @pl.when((window == 1) & six)
+        def _():
+            give_on(band).start()
+
+    step(only, 0)
+
+    @pl.when(six & middle_rows)
+    def _():
+        step(1, 0)
+
+    step(only, 1)
+
+    @pl.when(six)
+    def _():
+        lax.fori_loop(middle_rows.astype(jnp.int32), 2, lambda turn, carry: (step(1, turn), carry)[1], 0)
 
     for load in loads[5:]:
         load.wait()
+    kept = 6 * (1 - only)
     early[...] = feed_forward(
-        jnp.concatenate([flat(made[0, 0, :, 6:12]), flat(made[0, 1, :, 6:12])], axis=0), xv[:, 0:6], w_out, gain_mlp, w_up, w_down
+        jnp.concatenate([flat(made[only, band, :, pl.ds(kept, 6)]) for band in range(2)], axis=0),
+        xv[:, pl.ds(6 * only, 6)],
+        w_out,
+        gain_mlp,
+        w_up,
+        w_down,
     )
 
-    @pl.when(seven)
+    @pl.when(six)
     def _():
         for band in range(2):
             late[3 * band : 3 * band + 3] = made[1, band, :, 0:6]
 
-    @pl.when(jnp.logical_not(seven))
+    @pl.when(jnp.logical_not(six))
     def _():
         for band in range(2):
             give_back(band).wait_recv()
             late[3 * band : 3 * band + 3] = got[band]
 
-    to_east.wait_send()
-
-    @pl.when(eight)
-    def _():
-        to_west.wait_send()
-
-    for present, _, _, _, copies, copies_2 in ways:
-
-        @pl.when(present)
-        def _():
-            for copy in copies:
-                copy.wait_send()
-
-        @pl.when(present & seven)
-        def _():
-            copies_2[0].wait_send()
-
-        @pl.when(present & eight)
-        def _():
-            copies_2[1].wait_send()
-
-    @pl.when(jnp.logical_not(eight))
-    def _():
-        give_back(0).wait_send()
-        give_back(1).wait_send()
+    def sent(condition, copy):
+        @pl.when(condition)
+        def _():
+            copy.wait_send()
+
+    sent(jnp.logical_not(six), to_east)
+    sent(pushes, to_west)
+    for present, _, copies, copies_2 in ways:
+        sent(present & jnp.logical_not(seven), copies[0])
+        sent(present & jnp.logical_not(six), copies[1])
+        sent(present & wider, copies_2[0])
+        sent(present & pushes, copies_2[1])
+    for band in range(2):
+        sent(jnp.logical_not(pushes), give_back(band))
+        sent(six, give_on(band))
 
 
 def solution(mesh):
@@ -425,15 +460,15 @@
                 pltpu.VMEM((2, 2, 3, 12, 4, D), BF16),
                 pltpu.VMEM((2, 2, 3, 144, D), F32),
                 pltpu.VMEM((2, 3, 6, 4, D), BF16),
-                pltpu.VMEM((2, 2, 288, 144), F32),
+                pltpu.VMEM((2, 2, 144, 144), F32),
                 pltpu.VMEM((D, 3 * D), BF16),
                 pltpu.SemaphoreType.DMA((10,)),
                 pltpu.SemaphoreType.DMA((10,)),
-                pltpu.SemaphoreType.DMA((2,)),
+                pltpu.SemaphoreType.DMA((4,)),
                 pltpu.SemaphoreType.DMA((2,)),
                 pltpu.SemaphoreType.DMA((6,)),
                 pltpu.SemaphoreType.DMA((3,)),
-                pltpu.SemaphoreType.REGULAR((3,)),
+                pltpu.SemaphoreType.REGULAR((2,)),
             ],
             compiler_params=pltpu.CompilerParams(
                 collective_id=0, has_side_effects=True, vmem_limit_bytes=40 * 1024 * 1024
@@ -441,7 +476,7 @@
             cost_estimate=pl.CostEstimate(flops=1_800_000_000, bytes_accessed=7_000_000, transcendentals=1_000_000),
         )(*held)
         out = pl.pallas_call(
-            finish,
+            functools.partial(finish, n_lon),
             out_shape=jax.ShapeDtypeStruct(x.shape, BF16),
             in_specs=[vmem] * 7,
             out_specs=hbm,

time: 18.4 us -> 17.7 us (0.962)
  Pallas kernels: 18.3 us -> 17.5 us
    pallas_call x1, Pallas kernels: 16.2 us -> 15.5 us  [body(): pl.pallas_call(functools.partial(kernel, n_lat, n_lon), out_shape=[half,...]
where the time goes in v5:
time: 17.7 us; the launch traced here: 17.5 us
  Pallas kernels  17.5 us (99%)
    pallas_call x1, Pallas kernels, body(): pl.pallas_call(functools.partial(kernel, n_lat, n_lon), out_shape=[half,...  15.5 us
    pallas_call x1, Pallas kernels, body(): pl.pallas_call(functools.partial(finish, n_lon), out_shape=jax.ShapeDtype...  2.07 us

profile of v5, /device:TPU:103, one launch (start us, length us, event | category | flops | bytes accessed | tf_op | source)
XLA Modules:
  0.0 17.5 jit_solution(10666163677028323028)
XLA Ops:
  0.0 15.5 %shard_map.73 = (bf16[6,6,4,512]{3,2,1,0:T(4,128)(2,1)S(1)}, bf16[6,6,4,512]{3,2,1,0:T(4,128)(2,1)S(1)}, bf16[6,12,4,512]{3,2,1,0:T(4,128)(2,1)S(1)}, bf16[512,5...) custom-call(bf16[6,12,4,512]{3,2,1,0:T(4,128)(2,1)} %bitcast.4, ...), custom_call_target="tpu_custom_call" | custom-call | flops 1800000000 | bytes 7000000 | tf_op jit(solution)/shard_map/pallas_call | solution.py:452
  15.5 2.1 %shard_map.74 = bf16[6,12,4,512]{3,2,1,0:T(4,128)(2,1)} custom-call(bf16[6,6,4,512]{3,2,1,0:T(4,128)(2,1)S(1)} %get-tuple-element.12.early, bf16[6,6,4,512]{3,2,1,0:T(4,128)(2,1)S(1)} %get-tuple-element.13.late, bf16[6,12,4,512]{3,2,1,0:T(4,128)(2,1)S(1)} %get-tuple-element.14.xv, bf16[512,512]{1,0:T(8,128)(2,1)S(1)} %get-tuple-element.15.w_out, ...), custom_call_target="tpu_custom_call" | custom-call | flops 700000000 | bytes 300000 | tf_op jit(solution)/shard_map/pallas_call | solution.py:478

commit v6 on v5

--- a/solution.py
+++ b/solution.py
@@ -74,14 +74,26 @@
 
 
 def finish(n_lon, early, late, xv, w_out, gain, w_up, w_down, o_hbm, done, sem):
-    eastern = 6 * (lax.rem(lax.axis_index("lon"), n_lon // 2) == n_lon // 4 - 1).astype(jnp.int32)
+    place = lax.rem(lax.axis_index("lon"), n_lon // 2)
+    eastern = 6 * (place == n_lon // 4 - 1).astype(jnp.int32)
+    whole = place == 0
     put = pltpu.make_async_copy(early, o_hbm.at[:, pl.ds(eastern, 6)], sem.at[0])
     put.start()
-    done[...] = feed_forward(flat(late[...]), xv[:, pl.ds(6 - eastern, 6)], w_out, gain, w_up, w_down)
-    last = pltpu.make_async_copy(done, o_hbm.at[:, pl.ds(6 - eastern, 6)], sem.at[1])
-    last.start()
+
+    def last(src):
+        return pltpu.make_async_copy(src, o_hbm.at[:, pl.ds(6 - eastern, 6)], sem.at[1])
+
+    @pl.when(whole)
+    def _():
+        last(late).start()
+
+    @pl.when(jnp.logical_not(whole))
+    def _():
+        done[...] = feed_forward(flat(late[...]), xv[:, pl.ds(6 - eastern, 6)], w_out, gain, w_up, w_down)
+        last(done).start()
+
     put.wait()
-    last.wait()
+    last(done).wait()
 
 
 def kernel(
@@ -237,7 +249,14 @@
         def _():
             pl.semaphore_signal(ok_sem.at[1], inc=1, device_id={"lat": lat, "lon": west}, device_id_type=MESH)
 
-        straight(True)
+        @pl.when(first_place)
+        def _():
+            corner(True)
+
+        @pl.when(jnp.logical_not(first_place))
+        def _():
+            straight(True)
+
         straight(False)
 
         @pl.when(jnp.logical_not(six))
@@ -248,8 +267,15 @@
         def _():
             to_west.start()
 
-        corner(True)
+        @pl.when(jnp.logical_not(first_place))
+        def _():
+            corner(True)
+
         corner(False)
+
+        @pl.when(first_place)
+        def _():
+            straight(True)
 
     @pl.when(last_place)
     def _():
@@ -269,11 +295,19 @@
             to_west.start()
 
         pl.semaphore_wait(ok_sem.at[0], 1)
+
+        @pl.when(place == 1)
+        def _():
+            straight(True)
+
         straight(False)
         pl.semaphore_wait(ok_sem.at[1], 1)
         corner(True)
         corner(False)
-        straight(True)
+
+        @pl.when(place != 1)
+        def _():
+            straight(True)
 
     key = lax.broadcasted_iota(jnp.int32, (144, 144), 1)
     query = lax.broadcasted_iota(jnp.int32, (144, 144), 0)
@@ -310,13 +344,12 @@
             device_id_type=MESH,
         )
 
-    for load in loads[:5]:
+    for load in loads:
         load.wait()
 
     low = lax.broadcasted_iota(jnp.int32, (72, 128), 1) < HEAD_DIM
     first = (lat >= middle).astype(jnp.int32)
     only = seven.astype(jnp.int32)
-    middle_rows = far_north | far_south
 
     def project(block):
         normed = norm32(flat(block).astype(F32), gain_attn[...])
@@ -340,7 +373,7 @@
     def step(window, turn):
         band = lax.rem(first + turn, 2)
 
-        @pl.when(turn == 0)
+        @pl.when((turn == 0) & ((window == 0) | seven))
         def _():
             own_rows(window)
 
@@ -385,18 +418,16 @@
 
     step(only, 0)
 
-    @pl.when(six & middle_rows)
-    def _():
-        step(1, 0)
+    @pl.when(six)
+    def _():
+        own_rows(1)
 
     step(only, 1)
 
     @pl.when(six)
     def _():
-        lax.fori_loop(middle_rows.astype(jnp.int32), 2, lambda turn, carry: (step(1, turn), carry)[1], 0)
-
-    for load in loads[5:]:
-        load.wait()
+        lax.fori_loop(0, 2, lambda turn, carry: (step(1, turn), carry)[1], 0)
+
     kept = 6 * (1 - only)
     early[...] = feed_forward(
         jnp.concatenate([flat(made[only, band, :, pl.ds(kept, 6)]) for band in range(2)], axis=0),
@@ -416,7 +447,17 @@
     def _():
         for band in range(2):
             give_back(band).wait_recv()
+
+    @pl.when(jnp.logical_not(six | first_place))
+    def _():
+        for band in range(2):
             late[3 * band : 3 * band + 3] = got[band]
+
+    @pl.when(first_place)
+    def _():
+        late[...] = feed_forward(
+            jnp.concatenate([flat(got[0]), flat(got[1])], axis=0), xv[:, 6:12], w_out, gain_mlp, w_up, w_down
+        )
 
     def sent(condition, copy):
         @pl.when(condition)

time: 17.7 us -> 17.6 us (level)
  no operation moved by 1% of the time
where the time goes in v6:
time: 17.6 us
  Pallas kernels  17.6 us (100%)
    pallas_call x1, Pallas kernels, body(): pl.pallas_call(functools.partial(kernel, n_lat, n_lon), out_shape=[half,...  15.5 us
    pallas_call x1, Pallas kernels, body(): pl.pallas_call(functools.partial(finish, n_lon), out_shape=jax.ShapeDtype...  2.09 us

profile of v6, /device:TPU:103, one launch (start us, length us, event | category | flops | bytes accessed | tf_op | source)
XLA Modules:
  0.0 17.6 jit_solution(12707311697554247186)
XLA Ops:
  0.0 15.5 %shard_map.73 = (bf16[6,6,4,512]{3,2,1,0:T(4,128)(2,1)S(1)}, bf16[6,6,4,512]{3,2,1,0:T(4,128)(2,1)S(1)}, bf16[6,12,4,512]{3,2,1,0:T(4,128)(2,1)S(1)}, bf16[512,5...) custom-call(bf16[6,12,4,512]{3,2,1,0:T(4,128)(2,1)} %bitcast.4, ...), custom_call_target="tpu_custom_call" | custom-call | flops 1800000000 | bytes 7000000 | tf_op jit(solution)/shard_map/pallas_call | solution.py:493
  15.5 2.1 %shard_map.74 = bf16[6,12,4,512]{3,2,1,0:T(4,128)(2,1)} custom-call(bf16[6,6,4,512]{3,2,1,0:T(4,128)(2,1)S(1)} %get-tuple-element.12.early, bf16[6,6,4,512]{3,2,1,0:T(4,128)(2,1)S(1)} %get-tuple-element.13.late, bf16[6,12,4,512]{3,2,1,0:T(4,128)(2,1)S(1)} %get-tuple-element.14.xv, bf16[512,512]{1,0:T(8,128)(2,1)S(1)} %get-tuple-element.15.w_out, ...), custom_call_target="tpu_custom_call" | custom-call | flops 700000000 | bytes 300000 | tf_op jit(solution)/shard_map/pallas_call | solution.py:519

commit v7 on v6

--- a/solution.py
+++ b/solution.py
@@ -227,13 +227,13 @@
     def corner(far):
         for present, is_far, copies, copies_2 in ways:
 
+            @pl.when(present & pushes & (is_far == far))
+            def _():
+                copies_2[1].start()
+
             @pl.when(present & (is_far == far) & jnp.logical_not(six))
             def _():
                 copies[1].start()
-
-            @pl.when(present & pushes & (is_far == far))
-            def _():
-                copies_2[1].start()
 
     greetings = 1 + ((even & jnp.logical_not(first_place)) | seven).astype(jnp.int32)
     for present, *_ in ways:
@@ -249,6 +249,10 @@
         def _():
             pl.semaphore_signal(ok_sem.at[1], inc=1, device_id={"lat": lat, "lon": west}, device_id_type=MESH)
 
+        @pl.when(eight)
+        def _():
+            to_west.start()
+
         @pl.when(first_place)
         def _():
             corner(True)
@@ -262,10 +266,6 @@
         @pl.when(jnp.logical_not(six))
         def _():
             to_east.start()
-
-        @pl.when(eight)
-        def _():
-            to_west.start()
 
         @pl.when(jnp.logical_not(first_place))
         def _():
@@ -438,27 +438,6 @@
         w_down,
     )
 
-    @pl.when(six)
-    def _():
-        for band in range(2):
-            late[3 * band : 3 * band + 3] = made[1, band, :, 0:6]
-
-    @pl.when(jnp.logical_not(six))
-    def _():
-        for band in range(2):
-            give_back(band).wait_recv()
-
-    @pl.when(jnp.logical_not(six | first_place))
-    def _():
-        for band in range(2):
-            late[3 * band : 3 * band + 3] = got[band]
-
-    @pl.when(first_place)
-    def _():
-        late[...] = feed_forward(
-            jnp.concatenate([flat(got[0]), flat(got[1])], axis=0), xv[:, 6:12], w_out, gain_mlp, w_up, w_down
-        )
-
     def sent(condition, copy):
         @pl.when(condition)
         def _():
@@ -472,8 +451,32 @@
         sent(present & wider, copies_2[0])
         sent(present & pushes, copies_2[1])
     for band in range(2):
-        sent(jnp.logical_not(pushes), give_back(band))
+        sent(jnp.logical_not(pushes | first_place), give_back(band))
         sent(six, give_on(band))
+
+    @pl.when(six)
+    def _():
+        for band in range(2):
+            late[3 * band : 3 * band + 3] = made[1, band, :, 0:6]
+
+    @pl.when(jnp.logical_not(six))
+    def _():
+        for band in range(2):
+            give_back(band).wait_recv()
+
+    @pl.when(jnp.logical_not(six | first_place))
+    def _():
+        for band in range(2):
+            late[3 * band : 3 * band + 3] = got[band]
+
+    @pl.when(first_place)
+    def _():
+        late[...] = feed_forward(
+            jnp.concatenate([flat(got[0]), flat(got[1])], axis=0), xv[:, 6:12], w_out, gain_mlp, w_up, w_down
+        )
+
+    for band in range(2):
+        sent(first_place, give_back(band))
 
 
 def solution(mesh):

time: 17.6 us -> 17.6 us (level)
  no operation moved by 1% of the time
where the time goes in v7:
time: 17.6 us; the launch traced here: 17.5 us
  Pallas kernels  17.5 us (99%)
    pallas_call x1, Pallas kernels, body(): pl.pallas_call(functools.partial(kernel, n_lat, n_lon), out_shape=[half,...  15.4 us
    pallas_call x1, Pallas kernels, body(): pl.pallas_call(functools.partial(finish, n_lon), out_shape=jax.ShapeDtype...  2.09 us

profile of v7, /device:TPU:103, one launch (start us, length us, event | category | flops | bytes accessed | tf_op | source)
XLA Modules:
  0.0 17.5 jit_solution(7223966567145767864)
XLA Ops:
  0.0 15.4 %shard_map.73 = (bf16[6,6,4,512]{3,2,1,0:T(4,128)(2,1)S(1)}, bf16[6,6,4,512]{3,2,1,0:T(4,128)(2,1)S(1)}, bf16[6,12,4,512]{3,2,1,0:T(4,128)(2,1)S(1)}, bf16[512,5...) custom-call(bf16[6,12,4,512]{3,2,1,0:T(4,128)(2,1)} %bitcast.4, ...), custom_call_target="tpu_custom_call" | custom-call | flops 1800000000 | bytes 7000000 | tf_op jit(solution)/shard_map/pallas_call | solution.py:496
  15.4 2.1 %shard_map.74 = bf16[6,12,4,512]{3,2,1,0:T(4,128)(2,1)} custom-call(bf16[6,6,4,512]{3,2,1,0:T(4,128)(2,1)S(1)} %get-tuple-element.12.early, bf16[6,6,4,512]{3,2,1,0:T(4,128)(2,1)S(1)} %get-tuple-element.13.late, bf16[6,12,4,512]{3,2,1,0:T(4,128)(2,1)S(1)} %get-tuple-element.14.xv, bf16[512,512]{1,0:T(8,128)(2,1)S(1)} %get-tuple-element.15.w_out, ...), custom_call_target="tpu_custom_call" | custom-call | flops 700000000 | bytes 300000 | tf_op jit(solution)/shard_map/pallas_call | solution.py:522

commit v8 on v7

--- a/solution.py
+++ b/solution.py
@@ -67,21 +67,23 @@
 
 
 def feed_forward(attended, x, w_out, gain, w_up, w_down):
-    residual = (flat(x).astype(F32) + dot(attended, w_out[...])).astype(BF16).astype(F32)
+    residual = (x.astype(F32) + dot(attended, w_out[...])).astype(BF16).astype(F32)
     hidden = gelu(dot(norm(residual, gain[...]), w_up[...])).astype(BF16)
-    block = (residual + dot(hidden, w_down[...])).astype(BF16)
-    return block.reshape(x.shape)
+    return (residual + dot(hidden, w_down[...])).astype(BF16)
+
+
+def has_whole(lon, n_lon):
+    place = lax.rem(lon, n_lon // 2)
+    return (place == 0) | (place == n_lon // 4 - 1)
 
 
 def finish(n_lon, early, late, xv, w_out, gain, w_up, w_down, o_hbm, done, sem):
-    place = lax.rem(lax.axis_index("lon"), n_lon // 2)
-    eastern = 6 * (place == n_lon // 4 - 1).astype(jnp.int32)
-    whole = place == 0
-    put = pltpu.make_async_copy(early, o_hbm.at[:, pl.ds(eastern, 6)], sem.at[0])
+    whole = has_whole(lax.axis_index("lon"), n_lon)
+    put = pltpu.make_async_copy(early, o_hbm.at[:, 0:6], sem.at[0])
     put.start()
 
     def last(src):
-        return pltpu.make_async_copy(src, o_hbm.at[:, pl.ds(6 - eastern, 6)], sem.at[1])
+        return pltpu.make_async_copy(src, o_hbm.at[:, 6:12], sem.at[1])
 
     @pl.when(whole)
     def _():
@@ -89,7 +91,7 @@
 
     @pl.when(jnp.logical_not(whole))
     def _():
-        done[...] = feed_forward(flat(late[...]), xv[:, pl.ds(6 - eastern, 6)], w_out, gain, w_up, w_down)
+        done[...] = feed_forward(flat(late[...]), flat(xv[:, 6:12]), w_out, gain, w_up, w_down).reshape(done.shape)
         last(done).start()
 
     put.wait()
@@ -428,15 +430,12 @@
     def _():
         lax.fori_loop(0, 2, lambda turn, carry: (step(1, turn), carry)[1], 0)
 
-    kept = 6 * (1 - only)
-    early[...] = feed_forward(
-        jnp.concatenate([flat(made[only, band, :, pl.ds(kept, 6)]) for band in range(2)], axis=0),
-        xv[:, pl.ds(6 * only, 6)],
-        w_out,
-        gain_mlp,
-        w_up,
-        w_down,
-    )
+    whole = has_whole(lon, n_lon)
+
+    @pl.when(jnp.logical_not(whole))
+    def _():
+        attended = jnp.concatenate([flat(made[0, band, :, 6:12]) for band in range(2)], axis=0)
+        early[...] = feed_forward(attended, flat(xv[:, 0:6]), w_out, gain_mlp, w_up, w_down).reshape(early.shape)
 
     def sent(condition, copy):
         @pl.when(condition)
@@ -464,16 +463,29 @@
         for band in range(2):
             give_back(band).wait_recv()
 
-    @pl.when(jnp.logical_not(six | first_place))
+    @pl.when(jnp.logical_not(six | seven))
     def _():
         for band in range(2):
             late[3 * band : 3 * band + 3] = got[band]
 
     @pl.when(first_place)
     def _():
-        late[...] = feed_forward(
-            jnp.concatenate([flat(got[0]), flat(got[1])], axis=0), xv[:, 6:12], w_out, gain_mlp, w_up, w_down
-        )
+        for band in range(2):
+            early[3 * band : 3 * band + 3] = made[0, band, :, 6:12]
+
+    @pl.when(seven)
+    def _():
+        for band in range(2):
+            early[3 * band : 3 * band + 3] = got[band]
+            late[3 * band : 3 * band + 3] = made[1, band, :, 0:6]
+
+    @pl.when(whole)
+    def _():
+        attended = jnp.concatenate([flat(early[...]), flat(late[...])], axis=0)
+        x = jnp.concatenate([flat(xv[:, 0:6]), flat(xv[:, 6:12])], axis=0)
+        values = feed_forward(attended, x, w_out, gain_mlp, w_up, w_down)
+        early[...] = values[0:144].reshape(early.shape)
+        late[...] = values[144:288].reshape(late.shape)
 
     for band in range(2):
         sent(first_place, give_back(band))

time: 17.6 us -> 17.1 us (0.972)
  Pallas kernels: 17.5 us -> 17 us
    pallas_call x1, Pallas kernels: 2.09 us -> 0.73 us  [body(): pl.pallas_call(functools.partial(finish, n_lon), out_shape=jax.ShapeDtype...]
    pallas_call x1, Pallas kernels: 15.4 us -> 16.2 us  [body(): pl.pallas_call(functools.partial(kernel, n_lat, n_lon), out_shape=[half,...]
where the time goes in v8:
time: 17.1 us; the launch traced here: 17 us
  Pallas kernels  17 us (99%)
    pallas_call x1, Pallas kernels, body(): pl.pallas_call(functools.partial(kernel, n_lat, n_lon), out_shape=[half,...  16.2 us
    pallas_call x1, Pallas kernels, body(): pl.pallas_call(functools.partial(finish, n_lon), out_shape=jax.ShapeDtype...  0.73 us

profile of v8, /device:TPU:103, one launch (start us, length us, event | category | flops | bytes accessed | tf_op | source)
XLA Modules:
  0.0 17.0 jit_solution(18428978933670819415)
XLA Ops:
  0.0 16.2 %shard_map.73 = (bf16[6,6,4,512]{3,2,1,0:T(4,128)(2,1)S(1)}, bf16[6,6,4,512]{3,2,1,0:T(4,128)(2,1)S(1)}, bf16[6,12,4,512]{3,2,1,0:T(4,128)(2,1)S(1)}, bf16[512,5...) custom-call(bf16[6,12,4,512]{3,2,1,0:T(4,128)(2,1)} %bitcast.4, ...), custom_call_target="tpu_custom_call" | custom-call | flops 1800000000 | bytes 7000000 | tf_op jit(solution)/shard_map/pallas_call | solution.py:508
  16.2 0.7 %shard_map.74 = bf16[6,12,4,512]{3,2,1,0:T(4,128)(2,1)} custom-call(bf16[6,6,4,512]{3,2,1,0:T(4,128)(2,1)S(1)} %get-tuple-element.12.early, bf16[6,6,4,512]{3,2,1,0:T(4,128)(2,1)S(1)} %get-tuple-element.13.late, bf16[6,12,4,512]{3,2,1,0:T(4,128)(2,1)S(1)} %get-tuple-element.14.xv, bf16[512,512]{1,0:T(8,128)(2,1)S(1)} %get-tuple-element.15.w_out, ...), custom_call_target="tpu_custom_call" | custom-call | flops 700000000 | bytes 300000 | tf_op jit(solution)/shard_map/pallas_call | solution.py:534

commit v9 on v8

--- a/solution.py
+++ b/solution.py
@@ -134,6 +134,8 @@
     lon = lax.axis_index("lon")
     west = lax.rem(lon + n_lon - 1, n_lon)
     east = lax.rem(lon + 1, n_lon)
+    north = lax.rem(lat + n_lat - 1, n_lat)
+    south = lax.rem(lat + 1, n_lat)
     has_north = lat > 0
     has_south = lat < n_lat - 1
 
@@ -156,7 +158,7 @@
     def _():
         greet(lat, east)
 
-    for present, other in ((has_north, lat - 1), (has_south, lat + 1)):
+    for present, other in ((has_north, north), (has_south, south)):
 
         @pl.when(present & even)
         def _():
@@ -196,21 +198,21 @@
 
     to_east = send(0, x_hbm.at[:, 6:12], halo.at[0, 3:9, 0:6], lat, east)
     to_north = [
-        send(1, x_hbm.at[0:3, 0:6], halo.at[0, 9:12, 6:12], lat - 1, lon),
-        send(2, x_hbm.at[0:3, 6:12], halo.at[0, 9:12, 0:6], lat - 1, east),
+        send(1, x_hbm.at[0:3, 0:6], halo.at[0, 9:12, 6:12], north, lon),
+        send(2, x_hbm.at[0:3, 6:12], halo.at[0, 9:12, 0:6], north, east),
     ]
     to_south = [
-        send(3, x_hbm.at[3:6, 0:6], halo.at[0, 0:3, 6:12], lat + 1, lon),
-        send(4, x_hbm.at[3:6, 6:12], halo.at[0, 0:3, 0:6], lat + 1, east),
+        send(3, x_hbm.at[3:6, 0:6], halo.at[0, 0:3, 6:12], south, lon),
+        send(4, x_hbm.at[3:6, 6:12], halo.at[0, 0:3, 0:6], south, east),
     ]
     to_west = send(5, x_hbm.at[:, 0:6], halo.at[1, 3:9, 6:12], lat, west)
     to_north_2 = [
-        send(6, x_hbm.at[0:3, 6:12], halo.at[1, 9:12, 0:6], lat - 1, lon),
-        send(7, x_hbm.at[0:3, 0:6], halo.at[1, 9:12, 6:12], lat - 1, west),
+        send(6, x_hbm.at[0:3, 6:12], halo.at[1, 9:12, 0:6], north, lon),
+        send(7, x_hbm.at[0:3, 0:6], halo.at[1, 9:12, 6:12], north, west),
     ]
     to_south_2 = [
-        send(8, x_hbm.at[3:6, 6:12], halo.at[1, 0:3, 0:6], lat + 1, lon),
-        send(9, x_hbm.at[3:6, 0:6], halo.at[1, 0:3, 6:12], lat + 1, west),
+        send(8, x_hbm.at[3:6, 6:12], halo.at[1, 0:3, 0:6], south, lon),
+        send(9, x_hbm.at[3:6, 0:6], halo.at[1, 0:3, 6:12], south, west),
     ]
 
     ways = ((has_north, far_north, to_north, to_north_2), (has_south, far_south, to_south, to_south_2))

time: 17.1 us -> 17.1 us (level)
  no operation moved by 1% of the time
where the time goes in v9:
time: 17.1 us; the launch traced here: 17 us
  Pallas kernels  17 us (99%)
    pallas_call x1, Pallas kernels, body(): pl.pallas_call(functools.partial(kernel, n_lat, n_lon), out_shape=[half,...  16.2 us
    pallas_call x1, Pallas kernels, body(): pl.pallas_call(functools.partial(finish, n_lon), out_shape=jax.ShapeDtype...  0.73 us

profile of v9, /device:TPU:103, one launch (start us, length us, event | category | flops | bytes accessed | tf_op | source)
XLA Modules:
  0.0 17.0 jit_solution(718927149183241847)
XLA Ops:
  0.0 16.2 %shard_map.73 = (bf16[6,6,4,512]{3,2,1,0:T(4,128)(2,1)S(1)}, bf16[6,6,4,512]{3,2,1,0:T(4,128)(2,1)S(1)}, bf16[6,12,4,512]{3,2,1,0:T(4,128)(2,1)S(1)}, bf16[512,5...) custom-call(bf16[6,12,4,512]{3,2,1,0:T(4,128)(2,1)} %bitcast.4, ...), custom_call_target="tpu_custom_call" | custom-call | flops 1800000000 | bytes 7000000 | tf_op jit(solution)/shard_map/pallas_call | solution.py:510
  16.2 0.7 %shard_map.74 = bf16[6,12,4,512]{3,2,1,0:T(4,128)(2,1)} custom-call(bf16[6,6,4,512]{3,2,1,0:T(4,128)(2,1)S(1)} %get-tuple-element.12.early, bf16[6,6,4,512]{3,2,1,0:T(4,128)(2,1)S(1)} %get-tuple-element.13.late, bf16[6,12,4,512]{3,2,1,0:T(4,128)(2,1)S(1)} %get-tuple-element.14.xv, bf16[512,512]{1,0:T(8,128)(2,1)S(1)} %get-tuple-element.15.w_out, ...), custom_call_target="tpu_custom_call" | custom-call | flops 700000000 | bytes 300000 | tf_op jit(solution)/shard_map/pallas_call | solution.py:536

commit v10 on v9

--- a/solution.py
+++ b/solution.py
@@ -231,7 +231,7 @@
     def corner(far):
         for present, is_far, copies, copies_2 in ways:
 
-            @pl.when(present & pushes & (is_far == far))
+            @pl.when(present & (seven | (eight & jnp.logical_not(is_far))) & (is_far == far))
             def _():
                 copies_2[1].start()
 
@@ -256,6 +256,12 @@
         @pl.when(eight)
         def _():
             to_west.start()
+
+        for present, is_far, copies, copies_2 in ways:
+
+            @pl.when(present & eight & is_far)
+            def _():
+                copies_2[1].start()
 
         @pl.when(first_place)
         def _():

time: 17.1 us -> 17.1 us (level)
  no operation moved by 1% of the time
where the time goes in v10:
time: 17.1 us; the launch traced here: 17 us
  Pallas kernels  17 us (99%)
    pallas_call x1, Pallas kernels, body(): pl.pallas_call(functools.partial(kernel, n_lat, n_lon), out_shape=[half,...  16.2 us
    pallas_call x1, Pallas kernels, body(): pl.pallas_call(functools.partial(finish, n_lon), out_shape=jax.ShapeDtype...  0.73 us

profile of v10, /device:TPU:103, one launch (start us, length us, event | category | flops | bytes accessed | tf_op | source)
XLA Modules:
  0.0 17.0 jit_solution(17787600402044952242)
XLA Ops:
  0.0 16.2 %shard_map.73 = (bf16[6,6,4,512]{3,2,1,0:T(4,128)(2,1)S(1)}, bf16[6,6,4,512]{3,2,1,0:T(4,128)(2,1)S(1)}, bf16[6,12,4,512]{3,2,1,0:T(4,128)(2,1)S(1)}, bf16[512,5...) custom-call(bf16[6,12,4,512]{3,2,1,0:T(4,128)(2,1)} %bitcast.4, ...), custom_call_target="tpu_custom_call" | custom-call | flops 1800000000 | bytes 7000000 | tf_op jit(solution)/shard_map/pallas_call | solution.py:516
  16.2 0.7 %shard_map.74 = bf16[6,12,4,512]{3,2,1,0:T(4,128)(2,1)} custom-call(bf16[6,6,4,512]{3,2,1,0:T(4,128)(2,1)S(1)} %get-tuple-element.12.early, bf16[6,6,4,512]{3,2,1,0:T(4,128)(2,1)S(1)} %get-tuple-element.13.late, bf16[6,12,4,512]{3,2,1,0:T(4,128)(2,1)S(1)} %get-tuple-element.14.xv, bf16[512,512]{1,0:T(8,128)(2,1)S(1)} %get-tuple-element.15.w_out, ...), custom_call_target="tpu_custom_call" | custom-call | flops 700000000 | bytes 300000 | tf_op jit(solution)/shard_map/pallas_call | solution.py:542

commit v11 on v9

--- a/solution.py
+++ b/solution.py
@@ -372,7 +372,8 @@
         for group in range(2):
             rows = tokens[144 * group : 144 * group + 144]
             for part in range(3):
-                own[window, group, part] = dot(rows, w_qkv[:, D * part : D * part + D])
+                scale = HEAD_DIM**-0.5 if part == 0 else 1.0
+                own[window, group, part] = dot(rows, w_qkv[:, D * part : D * part + D]) * scale
 
     def step(window, turn):
         band = lax.rem(first + turn, 2)
@@ -395,7 +396,7 @@
         for group in range(2):
             rows = slice(72 * group, 72 * group + 72)
             q, k_own, v_own = [own[window, group, part, pl.ds(72 * band, 72)] for part in range(3)]
-            q = (q * HEAD_DIM**-0.5).astype(BF16)
+            q = q.astype(BF16)
             k = jnp.concatenate([others[0][rows], k_own], axis=0).astype(BF16)
             v = jnp.concatenate([others[1][rows], v_own], axis=0).astype(BF16)
             parts = []

time: 17.1 us -> 17 us (level)
  no operation moved by 1% of the time
where the time goes in v11:
time: 17 us
  Pallas kernels  17 us (100%)
    pallas_call x1, Pallas kernels, body(): pl.pallas_call(functools.partial(kernel, n_lat, n_lon), out_shape=[half,...  16.2 us
    pallas_call x1, Pallas kernels, body(): pl.pallas_call(functools.partial(finish, n_lon), out_shape=jax.ShapeDtype...  0.73 us

profile of v11, /device:TPU:103, one launch (start us, length us, event | category | flops | bytes accessed | tf_op | source)
XLA Modules:
  0.0 17.0 jit_solution(879760322073984121)
XLA Ops:
  0.0 16.2 %shard_map.73 = (bf16[6,6,4,512]{3,2,1,0:T(4,128)(2,1)S(1)}, bf16[6,6,4,512]{3,2,1,0:T(4,128)(2,1)S(1)}, bf16[6,12,4,512]{3,2,1,0:T(4,128)(2,1)S(1)}, bf16[512,5...) custom-call(bf16[6,12,4,512]{3,2,1,0:T(4,128)(2,1)} %bitcast.4, ...), custom_call_target="tpu_custom_call" | custom-call | flops 1800000000 | bytes 7000000 | tf_op jit(solution)/shard_map/pallas_call | solution.py:511
  16.2 0.7 %shard_map.74 = bf16[6,12,4,512]{3,2,1,0:T(4,128)(2,1)} custom-call(bf16[6,6,4,512]{3,2,1,0:T(4,128)(2,1)S(1)} %get-tuple-element.12.early, bf16[6,6,4,512]{3,2,1,0:T(4,128)(2,1)S(1)} %get-tuple-element.13.late, bf16[6,12,4,512]{3,2,1,0:T(4,128)(2,1)S(1)} %get-tuple-element.14.xv, bf16[512,512]{1,0:T(8,128)(2,1)S(1)} %get-tuple-element.15.w_out, ...), custom_call_target="tpu_custom_call" | custom-call | flops 700000000 | bytes 300000 | tf_op jit(solution)/shard_map/pallas_call | solution.py:537
